TPU v7x, 128 devices: a whole 4x4x4 slice. The times are simulated.
128 devices in a mesh: outer: 16 (over z, y), inner: 4 (over x_lo, core), head: 2 (over x_hi).
Axes of the slice: x: 4 (x_hi: 2, x_lo: 2; x = x_hi * 2 + x_lo), y: 4, z: 4, core: 2. Of those that a mesh axis runs over, the one named last changes fastest.
Arguments:
- queries: bfloat16 [16384, 4096], P(('outer', 'inner'), 'head'), may hold values from -6 to 6
- key_heads: bfloat16 [16384, 1024], P(('outer', 'inner', 'head')), may hold values from -6 to 6
- value_heads: bfloat16 [16384, 1024], P(('outer', 'inner', 'head')), may hold values from -6 to 6
- output: bfloat16 [16384, 4096], P(('outer', 'inner'), 'head'), may hold values from -1.5 to 1.5
- output_grad: bfloat16 [16384, 4096], P(('outer', 'inner'), 'head'), may hold values from -192 to 192
- log_totals: float32 [32, 16384], P('head', ('outer', 'inner')), may hold values from 7 to 8.5
- random_blocks: int32 [128, 3], P(('outer', 'inner')), may hold values from 0 to 127, as said below
- window_width: int32 [128], P(('outer', 'inner')), may hold values from 1 to 2, as said below
- global_blocks: int32 [2], replicated, may hold values from 0 to 127
Outputs:
- query_grad: bfloat16 [16384, 4096], P(('outer', 'inner'), 'head')
- key_grad: bfloat16 [16384, 1024], P(('outer', 'inner', 'head'))
- value_grad: bfloat16 [16384, 1024], P(('outer', 'inner', 'head'))
Inputs may be any that keep to these rules, and one draw needn't show every extreme that they name: `random_blocks`: number the sequence shards of 256 tokens s = 0, 1, ... The random key blocks of query blocks of shard s lie in shards s2 with s2 % 4 == s % 4; the 6 random entries of shard s name distinct key blocks, at most 2 of them in any one shard and exactly 2 in at least one. `window_width`: the value 2 occurs in every draw.
All inputs are finite; a program needn't handle non-finite values.
Results may differ from a plain program's by a relative error of at most 0.0053.
Values may be sent and summed in bfloat16 or wider, within the bound.
A program may use at most 128 MiB of HBM per device.

v0:
```python
import jax
import jax.numpy as jnp
from jax import lax
from jax.sharding import PartitionSpec as P

HDIM = 128
BLOCK = 128
WIN = 2
GLOB = 2
RAND = 3


def padded(cells, sides, width):
    for axis, dim in sides:
        count = lax.axis_size(axis)
        ends = count - 1
        head = lax.slice_in_dim(cells, 0, width, axis=dim)
        tail = lax.slice_in_dim(cells, cells.shape[dim] - width, cells.shape[dim], axis=dim)
        cells = jnp.concatenate(
            [
                lax.ppermute(tail, axis, [(i, (i + 1) % count) for i in range(ends)]),
                cells,
                lax.ppermute(head, axis, [((i + 1) % count, i) for i in range(ends)]),
            ],
            axis=dim,
        )
    return cells


def from_root(value, axis, root):
    mine = lax.axis_index(axis) == root
    return lax.psum(jnp.where(mine, value, jnp.zeros_like(value)), axis)


def on_device(
    queries,
    key_heads,
    value_heads,
    output,
    output_grad,
    log_totals,
    random_blocks,
    window_width,
    global_blocks,
):
    score_scale = HDIM ** (-0.5)
    tok_rows = queries.shape[0]
    block_count = tok_rows // BLOCK
    outer_size = lax.axis_size("outer")
    inner_size = lax.axis_size("inner")
    shard_total = outer_size * inner_size
    shard_index = lax.axis_index("outer") * inner_size + lax.axis_index("inner")
    window_span = 2 * WIN + 1
    list_length = window_span + GLOB + RAND
    rim_rows = WIN * BLOCK
    kv_pair = (
        lax.all_to_all(key_heads, "head", split_axis=1, concat_axis=0, tiled=True),
        lax.all_to_all(value_heads, "head", split_axis=1, concat_axis=0, tiled=True),
    )
    kv_local = jnp.stack(kv_pair)
    kv_width = kv_local.shape[2]
    kv_local_heads = kv_width // HDIM
    query_heads = queries.shape[1] // HDIM
    head_group = query_heads // kv_local_heads
    kv_blocks = kv_local.reshape(2, block_count, BLOCK, kv_width)
    extended = padded(kv_local, ((("outer", "inner"), 1),), rim_rows)
    ext_blocks = extended.reshape(2, block_count + 2 * WIN, BLOCK, kv_width)
    window_keys = jnp.stack(
        [
            ext_blocks[:, offset_index : offset_index + block_count]
            for offset_index in range(window_span)
        ],
        axis=2,
    )
    global_list = []
    for global_index in range(GLOB):
        block_id = global_blocks[global_index]
        global_piece = lax.dynamic_index_in_dim(
            kv_blocks, block_id % block_count, 1, keepdims=False
        )
        global_list.append(from_root(global_piece, ("outer", "inner"), block_id // block_count))
    global_keys = jnp.stack(global_list, axis=1)
    ref_blocks = random_blocks.reshape(-1)
    owner_index = ref_blocks // block_count // inner_size
    local_index = ref_blocks % block_count
    slot_cap = min(block_count, max(2, -(-(block_count * RAND) // outer_size)))
    owner_hits = (owner_index[:, None] == jnp.arange(outer_size)[None, :]).astype(jnp.int32)
    slot_rank = jnp.sum(jnp.cumsum(owner_hits, axis=0) * owner_hits, axis=1) - 1
    slot_index = owner_index * slot_cap + slot_rank
    wanted = jnp.zeros((outer_size * slot_cap,), jnp.int32).at[slot_index].set(local_index)
    asked_blocks = lax.all_to_all(
        wanted.reshape(outer_size, slot_cap), "outer", split_axis=0, concat_axis=0, tiled=True
    )
    ref_rows = owner_index * tok_rows + local_index * BLOCK
    zero_picks = jnp.zeros((2, block_count * RAND, BLOCK, kv_width), jnp.bfloat16)
    shard_piece = lax.all_gather(kv_local, "outer", axis=1, tiled=True)
    piece_blocks = shard_piece.shape[1] // BLOCK
    split_piece = shard_piece.reshape(2, piece_blocks, BLOCK, kv_width)
    inside = (ref_rows >= 0) & (ref_rows < shard_piece.shape[1])
    taken_blocks = jnp.take(split_piece, jnp.clip(ref_rows // BLOCK, 0, piece_blocks - 1), axis=1)
    rand_keys = jnp.where(inside[None, :, None, None], taken_blocks, zero_picks)
    all_keys = jnp.concatenate(
        [
            window_keys,
            jnp.broadcast_to(global_keys[:, None], (2, block_count, GLOB, BLOCK, kv_width)),
            rand_keys.reshape(2, block_count, RAND, BLOCK, kv_width),
        ],
        axis=2,
    )
    query_block_ids = shard_index * block_count + jnp.arange(block_count)
    window_offsets = jnp.arange(-WIN, WIN + 1)
    target = query_block_ids[:, None] + window_offsets[None, :]
    window_ok = (
        (jnp.abs(window_offsets)[None, :] <= window_width[:, None])
        & (target >= 0)
        & (target < block_count * shard_total)
    )
    entry_mask = jnp.concatenate(
        [window_ok, jnp.ones((block_count, GLOB + RAND), jnp.bool_)], axis=1
    )
    delta_rows = jnp.sum(
        output_grad.astype(jnp.float32).reshape(tok_rows, query_heads, HDIM)
        * output.astype(jnp.float32).reshape(tok_rows, query_heads, HDIM),
        axis=-1,
    )
    delta_blocks = jnp.transpose(delta_rows).reshape(query_heads, block_count, BLOCK)
    lse_blocks = log_totals.reshape(query_heads, block_count, BLOCK)
    query_parts = []
    key_parts = []
    value_parts = []
    for kv_head in range(kv_local_heads):
        lower = kv_head * head_group * HDIM
        upper = (kv_head + 1) * head_group * HDIM
        query_head = queries[:, lower:upper].reshape(block_count, BLOCK, head_group, HDIM)
        grad_head = output_grad[:, lower:upper].reshape(block_count, BLOCK, head_group, HDIM)
        key_tiles = all_keys[0, :, :, :, kv_head * HDIM : (kv_head + 1) * HDIM]
        value_tiles = all_keys[1, :, :, :, kv_head * HDIM : (kv_head + 1) * HDIM]
        lse_head = jnp.transpose(
            lse_blocks[kv_head * head_group : (kv_head + 1) * head_group], (1, 0, 2)
        )
        delta_head = jnp.transpose(
            delta_blocks[kv_head * head_group : (kv_head + 1) * head_group], (1, 0, 2)
        )
        scores = (
            jnp.einsum(
                "bqgd,bjkd->bgqjk", query_head, key_tiles, preferred_element_type=jnp.float32
            )
            * score_scale
        )
        probs = jnp.where(
            entry_mask[:, None, None, :, None], jnp.exp(scores - lse_head[:, :, :, None, None]), 0.0
        )
        probs_half = probs.astype(jnp.bfloat16)
        value_entry = jnp.einsum(
            "bgqjk,bqgd->bjkd", probs_half, grad_head, preferred_element_type=jnp.float32
        )
        prob_grad = jnp.einsum(
            "bqgd,bjkd->bgqjk", grad_head, value_tiles, preferred_element_type=jnp.float32
        )
        score_grad = (probs * (prob_grad - delta_head[:, :, :, None, None])).astype(jnp.bfloat16)
        query_part = (
            jnp.einsum(
                "bgqjk,bjkd->bqgd", score_grad, key_tiles, preferred_element_type=jnp.float32
            )
            * score_scale
        )
        key_entry = (
            jnp.einsum(
                "bgqjk,bqgd->bjkd", score_grad, query_head, preferred_element_type=jnp.float32
            )
            * score_scale
        )
        query_parts.append(query_part.reshape(tok_rows, head_group * HDIM))
        key_parts.append(key_entry)
        value_parts.append(value_entry)
    query_grad = jnp.concatenate(query_parts, axis=1).astype(jnp.bfloat16)
    entries = jnp.stack(
        [jnp.concatenate(key_parts, axis=-1), jnp.concatenate(value_parts, axis=-1)]
    )
    window_sums = jnp.zeros((2, block_count + 2 * WIN, BLOCK, kv_width), jnp.float32)
    for offset_index in range(window_span):
        window_sums = window_sums.at[:, offset_index : offset_index + block_count].add(
            entries[:, :, offset_index]
        )
    outgoing = jnp.concatenate([window_sums[:, :WIN], window_sums[:, WIN + block_count :]], axis=1)
    outgoing = outgoing.reshape(2, 2 * rim_rows, kv_width)
    rim_back = padded(outgoing, ((("outer", "inner"), 1),), rim_rows)
    owned_sums = window_sums[:, WIN : WIN + block_count].reshape(2, tok_rows, kv_width)
    owned_sums = owned_sums.at[:, :rim_rows].add(rim_back[:, :rim_rows])
    owned_sums = owned_sums.at[:, tok_rows - rim_rows :].add(rim_back[:, 3 * rim_rows :])
    owned_sums = owned_sums.reshape(2, block_count, BLOCK, kv_width)
    global_entry = jnp.sum(entries[:, :, window_span : window_span + GLOB], axis=1)
    global_total = lax.psum(global_entry, ("outer", "inner"))
    for global_index in range(GLOB):
        block_id = global_blocks[global_index]
        owner_hit = (block_id // block_count == shard_index) & (
            jnp.arange(block_count) == block_id % block_count
        )
        owned_sums = owned_sums + jnp.where(
            owner_hit[None, :, None, None], global_total[:, global_index][:, None], 0.0
        )
    random_entry = (
        entries[:, :, window_span + GLOB : list_length]
        .reshape(2, block_count * RAND, BLOCK, kv_width)
        .astype(jnp.bfloat16)
    )
    slots_out = (
        jnp.zeros((2, outer_size * slot_cap, BLOCK, kv_width), jnp.bfloat16)
        .at[:, slot_index]
        .set(random_entry)
    )
    returned_slots = lax.all_to_all(
        slots_out.reshape(2, outer_size, slot_cap, BLOCK, kv_width),
        "outer",
        split_axis=1,
        concat_axis=1,
        tiled=True,
    )
    returned_slots = returned_slots.reshape(2, outer_size * slot_cap, BLOCK, kv_width)
    pick_matrix = (asked_blocks.reshape(-1)[:, None] == jnp.arange(block_count)[None, :]).astype(
        jnp.bfloat16
    )
    rand_sum = jnp.einsum(
        "sb,xskd->xbkd", pick_matrix, returned_slots, preferred_element_type=jnp.float32
    )
    owned_sums = owned_sums + rand_sum
    kv_grads = owned_sums.reshape(2, tok_rows, kv_width).astype(jnp.bfloat16)
    grads_home = lax.all_to_all(kv_grads, "head", split_axis=1, concat_axis=2, tiled=True)
    return (query_grad, grads_home[0], grads_home[1])


def solution(mesh):
    placed = (
        P(("outer", "inner"), "head"),
        P(("outer", "inner", "head"), None),
        P(("outer", "inner", "head"), None),
        P(("outer", "inner"), "head"),
        P(("outer", "inner"), "head"),
        P("head", ("outer", "inner")),
        P(("outer", "inner"), None),
        P(("outer", "inner")),
        P(),
    )
    return jax.shard_map(
        on_device,
        mesh=mesh,
        in_specs=placed,
        out_specs=(
            P(("outer", "inner"), "head"),
            P(("outer", "inner", "head"), None),
            P(("outer", "inner", "head"), None),
        ),
        check_vma=False,
    )
```

profile of v0, /device:TPU:8, one launch (start us, length us, event | category | flops | bytes accessed | tf_op | source)
XLA Modules:
  0.0 1271.5 jit_solution(14540749675841974181)
XLA Ops:
  8.0 1.8 copy.430
  9.8 4.3 all-to-all-start
  14.1 1.8 copy.429
  15.8 4.9 all-to-all-done
  20.7 3.4 all-to-all-start.1
  24.3 1.3 fusion.140
  34.9 8.4 all-to-all-start.3
  52.5 1.6 multiply_bitcast_fusion
  57.0 1.9 collective-permute-start.1
  59.0 2.6 collective-permute-start
  62.4 511.1 %all-reduce.8.cloned.1.call-done = (bf16[2,1,128,512]{3,2,1,0:T(8,128)(2,1)}, bf16[2,1,128,512]{3,2,1,0:T(8,128)(2,1)}) async-done(((bf16[2,1,128,512]{3,2,1,0:T(8,128)(2,1)}, bf16[2,1,128,512]{3,2,1,0:T(8,128)(2,1)}), (bf16[2,1,128,512]{3,2,1,0:T(8,128)(2,1)}, bf16[2,1,128,512]{3,2,1,0:T(8,128)(2,1)})) %all-reduce.8.cloned.1.call-update) | async-done | bytes 524304 | tf_op jit(solution)/shard_map/psum | solution.py:32
  580.1 4.0 gather_fusion
  584.2 1.7 select_dynamic-update-slice_fusion
  585.9 1.9 fusion.100
  587.8 1.1 fusion.56
  588.9 2.6 fusion.1
  591.5 1.5 copy-done.5
  594.0 1.9 fusion.99
  596.0 1.1 fusion.53
  597.1 2.6 fusion.5
  599.7 1.5 copy-done.6
  602.2 1.9 fusion.98
  604.1 1.1 fusion.50
  605.2 2.6 fusion.9
  607.8 1.5 copy-done.7
  609.3 1.2 fusion.61
  610.5 1.9 fusion.97
  612.4 1.1 fusion.47
  613.6 2.6 fusion.13
  616.2 1.5 copy-done.4
  619.5 1.9 copy-done
  621.7 2.1 copy-done.1
  624.5 4.3 broadcast_in_dim.128
  628.8 4.8 scatter_fusion
  633.6 16.4 %copy.300 = bf16[2,16,2,128,512]{4,2,3,0,1:T(2,128)(2,1)} copy(bf16[2,16,2,128,512]{4,3,2,1,0:T(8,128)(2,1)} %bitcast.457) | data formatting | bytes 16777216 | tf_op jit(solution)/shard_map/reshape | solution.py:213
  650.0 9.9 all-to-all-start.2
  659.9 2.7 fusion.46
  662.7 1.4 fusion.76
  664.4 1.1 slice-done.1
  665.5 1.5 fusion.80
  667.9 1.5 copy-done.2
  669.4 1.5 pad_maximum_fusion.1
  670.9 1.9 copy.296
  672.8 1.5 fusion.135
  674.3 2.2 collective-permute-start.2
  676.5 4.8 collective-permute-start.3
  682.6 3.3 fusion.74
  685.8 3.3 fusion.73
  689.1 1.7 fusion.72
  690.8 10.1 collective-permute-done.2
  700.8 1.5 copy.297
  703.4 1.5 copy.298
  704.9 509.9 %all-reduce.6.cloned.1.call-done = f32[2,2,128,512]{2,3,1,0:T(8,128)} async-done(((f32[2,2,128,512]{2,3,1,0:T(8,128)}), f32[2,2,128,512]{2,3,1,0:T(8,128)}) %all-reduce.6.cloned.1.call-update) | async-done | bytes 1048592 | tf_op jit(solution)/shard_map/psum | solution.py:193
  1214.8 2.3 slice_bitcast_fusion.21
  1217.1 10.1 copy.301
  1227.2 13.1 %reshape.742 = bf16[2,32,128,512]{3,1,2,0:T(8,128)(2,1)} reshape(bf16[2,16,2,128,512]{4,2,1,3,0:T(2,128)(2,1)} %copy.301) | data formatting | bytes 16777216 | tf_op jit(solution)/shard_map/reshape | solution.py:219
  1240.3 4.6 fusion.111
  1244.9 1.3 copy.303
  1246.2 2.2 fusion.96
  1248.6 1.3 copy.305
  1249.9 4.0 all-to-all-start.4
  1253.8 2.5 fusion.71
  1257.4 1.1 pad_maximum_fusion.3
  1258.5 3.4 all-to-all-done.4
  (137 shorter events, 35.1 us)
Async XLA Ops:
  8.0 24.7 %copy-start.17 = (s32[2,3]{1,0:T(2,128)S(1)}, s32[2,3]{1,0:T(2,128)}, u32[]{:S(2)}) copy-start(s32[2,3]{1,0:T(2,128)} %param.33) | copy-start | bytes 76
  8.0 35.3 %copy-start.10 = (bf16[256,2048]{1,0:T(8,128)(2,1)S(1)}, bf16[256,2048]{1,0:T(8,128)(2,1)}, u32[]{:S(2)}) copy-start(bf16[256,2048]{1,0:T(8,128)(2,1)} %param.27) | copy-start | bytes 3145732
  9.8 11.0 all-to-all-start
  14.1 32.8 %copy-start.3 = (bf16[256,2048]{1,0:T(8,128)(2,1)S(1)}, bf16[256,2048]{1,0:T(8,128)(2,1)}, u32[]{:S(2)}) copy-start(bf16[256,2048]{1,0:T(8,128)(2,1)} %param.31) | copy-start | bytes 3145732
  20.7 10.1 all-to-all-start.1
  24.2 549.3 %all-reduce.8.cloned.1.call-start = ((), (), s32[]{:S(2)}) async-start(), calls=%async_computation.7 | async-start | bytes 1048576 | tf_op jit(solution)/shard_map/psum | solution.py:32
  31.7 548.3 %all-gather.2.cloned.1.call-start = ((), (), s32[]{:S(2)}) async-start(), calls=%async_computation.5 | async-start | bytes 8912896 | tf_op jit(solution)/shard_map/all_gather | solution.py:96
  32.8 10.6 copy-start.18
  34.9 615.1 %all-to-all-start.3 = ((s32[16,1,2]{2,1,0:T(1,128)}), s32[16,1,2]{2,1,0:T(1,128)S(1)}, u32[]{:S(2)}, u32[]{:S(2)}) async-start(s32[16,1,2]{2,1,0:T(1,128)} %bitcast.136), calls=%async_computation.3 | async-start | bytes 16384 | tf_op jit(solution)/shard_map/all_to_all | solution.py:91
  57.0 517.5 %collective-permute-start.1 = (bf16[2,256,512]{2,1,0:T(8,128)(2,1)}, bf16[2,256,512]{2,1,0:T(8,128)(2,1)S(1)}, u32[]{:S(2)}, u32[]{:S(2)}) collective-permute-start(bf16[2,256,512]{2,1,0:T(8,128)(2,1)} %pad_maximum_fusion.4), channel_id=1, source_target_pairs={{2,0},{4,2},{6,4},{8,6},{10,8},{12,10},{14,12},{16,14},{18,16},{20... | collective-permute-start | bytes 1572872 | tf_op jit(solution)/shard_map/ppermute | solution.py:23
  59.0 515.6 %collective-permute-start = (bf16[2,256,512]{2,1,0:T(8,128)(2,1)}, bf16[2,256,512]{2,1,0:T(8,128)(2,1)S(1)}, u32[]{:S(2)}, u32[]{:S(2)}) collective-permute-start(bf16[2,256,512]{2,1,0:T(8,128)(2,1)} %pad_maximum_fusion.4), channel_id=1, source_target_pairs={{0,2},{2,4},{4,6},{6,8},{8,10},{10,12},{12,14},{14,16},{16,18},{18... | collective-permute-start | bytes 1572872 | tf_op jit(solution)/shard_map/ppermute | solution.py:21
  579.0 6.9 copy-start.9
  584.2 3.6 copy-start.14
  591.5 1.5 copy-start.5
  593.0 2.9 copy-start.13
  599.7 1.5 copy-start.6
  601.2 2.9 copy-start.12
  607.8 1.5 copy-start.7
  609.3 3.1 copy-start.11
  616.2 1.5 copy-start.4
  619.1 2.3 copy-start
  621.4 2.4 copy-start.1
  650.0 567.1 %all-to-all-start.2 = ((bf16[2,16,2,128,512]{4,2,3,0,1:T(2,128)(2,1)}), bf16[2,16,2,128,512]{4,2,3,0,1:T(2,128)(2,1)}, u32[]{:S(2)}, u32[]{:S(2)}) async-start(bf16[2,16,2,128,512]{4,2,3,0,1:T(2,128)(2,1)} %copy.300), calls=%async_computation.2 | async-start | bytes 16777216 | tf_op jit(solution)/shard_map/all_to_all | solution.py:212
  659.9 555.0 %all-reduce.6.cloned.1.call-start = ((), (), s32[]{:S(2)}) async-start(), calls=%async_computation.6 | async-start | bytes 2097152 | tf_op jit(solution)/shard_map/psum | solution.py:193
  662.7 1.7 slice-start
  662.7 2.8 slice-start.1
  664.1 2.9 slice-start.2
  665.5 1.8 slice-start.3
  667.7 1.7 copy-start.2
  674.3 14.8 %copy-start.8 = (bf16[2,4,128,10,128]{2,4,1,3,0:T(8,128)(2,1)S(1)}, bf16[2,4,128,10,128]{2,4,1,3,0:T(8,128)(2,1)}, u32[]{:S(2)}) copy-start(bf16[2,4,128,10,128]{2,4,1,3,0:T(8,128)(2,1)} %copy-done.7) | copy-start | bytes 7864324
  674.3 26.6 %collective-permute-start.2 = (f32[2,256,512]{2,1,0:T(8,128)}, f32[2,256,512]{2,1,0:T(8,128)}, u32[]{:S(2)}, u32[]{:S(2)}) collective-permute-start(f32[2,256,512]{2,1,0:T(8,128)} %get-tuple-element.120), channel_id=1, source_target_pairs={{0,2},{2,4},{4,6},{6,8},{8,10},{10,12},{12,14},{14,16},{16,18},{18... | collective-permute-start | bytes 3145736 | tf_op jit(solution)/shard_map/ppermute | solution.py:21
  676.5 26.9 %collective-permute-start.3 = (f32[2,256,512]{2,1,0:T(8,128)}, f32[2,256,512]{2,1,0:T(8,128)}, u32[]{:S(2)}, u32[]{:S(2)}) collective-permute-start(f32[2,256,512]{2,1,0:T(8,128)} %get-tuple-element.121), channel_id=1, source_target_pairs={{2,0},{4,2},{6,4},{8,6},{10,8},{12,10},{14,12},{16,14},{18,16},{20... | collective-permute-start | bytes 3145736 | tf_op jit(solution)/shard_map/ppermute | solution.py:23
  1248.3 8.1 copy-start.16
  1248.3 8.3 copy-start.15
  1249.9 12.0 all-to-all-start.4
Sparse Core Ops, SparseCore 0:
  31.9 541.5 all-reduce.7
  663.3 551.4 all-reduce.5
Sparse Core Ops, SparseCore 1:
  35.2 73.6 all-gather.1
where the time goes:
time: 1280 us; the launch traced here: 1270 us
  waiting for transfers between devices  1040 us (81%)
  local copies, waits for them, and re-layouts  104 us (8%)
  matrix products  41.9 us (3%)
  starting transfers between devices  41.6 us (3%)
  other arithmetic  21.8 us (2%)
  between operations  21.5 us (2%)
    psum x1, waiting for transfers between devices, from_root(): return lax.psum(jnp.where(mine, value, jnp.zeros_like(value)), axis)  511 us
    psum x1, waiting for transfers between devices, on_device(): global_total = lax.psum(global_entry, ('outer', 'inner'))  510 us
  transfers between devices with their start and end apart: 12, of which 7 were waited for; matrix products, arithmetic and copies ran while one was open for 9% of the time, Pallas kernels for 0%

commit v1 on v0

v1 whole, which is shorter than its diff:
```python
import math

import jax
import jax.numpy as jnp
from jax import lax
from jax.experimental import pallas as pl
from jax.experimental.pallas import tpu as pltpu
from jax.sharding import PartitionSpec as P

MESH = pl.DeviceIdType.MESH
HDIM = 128
BLOCK = 128
NZ = 4
NY = 4
NI = 4
HALO = 32
GLOBAL = 48
SLOTS = 50
SCALE = HDIM ** (-0.5)
LOG2E = math.log2(math.e)
ZH = [(dz, dh) for dz in range(4) for dh in range(2) if (dz, dh) != (0, 0)]
BF = jnp.bfloat16
F32 = jnp.float32


def place():
    outer = lax.axis_index("outer")
    return outer // NY, lax.rem(outer, NY), lax.axis_index("inner"), lax.axis_index("head")


def device(z, y, i, h):
    return (z * NY + y, i, h)


def shifted(dz=0, dy=0, di=0, dh=0):
    z, y, i, h = place()
    return device(lax.rem(z + dz, NZ), lax.rem(y + dy, NY), lax.rem(i + di, NI), lax.rem(h + dh, 2))


def along(step):
    z, y, i, h = place()
    turn = lax.rem(y * NI + i + step + NY * NI, NY * NI)
    return device(z, turn // NI, lax.rem(turn, NI), h)


def peers():
    found = [shifted(dz=dz, dh=dh) for dz, dh in ZH]
    found += [shifted(dy=dy) for dy in range(1, NY)]
    found += [shifted(di=di) for di in range(1, NI)]
    found += [along(1), along(-1)]
    return found


def meet():
    barrier = pltpu.get_barrier_semaphore()
    found = peers()
    for one in found:
        pl.semaphore_signal(barrier, inc=1, device_id=one, device_id_type=MESH)
    pl.semaphore_wait(barrier, len(found))


def remote(src, dst, send, recv, to):
    return pltpu.make_async_remote_copy(
        src_ref=src, dst_ref=dst, send_sem=send, recv_sem=recv, device_id=to, device_id_type=MESH
    )


def columns(index, width):
    return pl.ds(pl.multiple_of(index * width, width), width)


def gather_kernel(
    glob_ref, q_ref, k_ref, v_ref, o_ref, g_ref, lse_ref, int_ref,
    qb, gb, kvu, stats, ints,
    og, sbuf, gsend, grecv,
    local_sem, kv_s, kv_r, q_s, q_r, st_s, st_r, it_s, it_r, ag_s, ag_r, hl_s, hl_r, gl_s, gl_r,
):
    z, y, i, h = place()
    loads = [
        pltpu.make_async_copy(o_ref, og.at[0], local_sem.at[0]),
        pltpu.make_async_copy(g_ref, og.at[1], local_sem.at[1]),
    ]
    own_col = columns(h * NZ + z, HDIM)
    own_slot = y * 8 + z * 2 + h
    keep = [
        pltpu.make_async_copy(k_ref.at[:, own_col], kvu.at[0, own_slot], local_sem.at[2]),
        pltpu.make_async_copy(v_ref.at[:, own_col], kvu.at[1, own_slot], local_sem.at[3]),
    ]
    stay = [
        pltpu.make_async_copy(q_ref.at[:, columns(z, 512)], qb.at[z], local_sem.at[4]),
        pltpu.make_async_copy(g_ref.at[:, columns(z, 512)], gb.at[z], local_sem.at[5]),
        pltpu.make_async_copy(int_ref, ints.at[z], local_sem.at[6]),
    ]
    for one in keep + loads + stay:
        one.start()
    meet()
    kv_copies = []
    for n, (dz, dh) in enumerate(ZH):
        to = shifted(dz=dz, dh=dh)
        col = columns(lax.rem(h + dh, 2) * NZ + lax.rem(z + dz, NZ), HDIM)
        for side, ref in enumerate((k_ref, v_ref)):
            kv_copies.append(
                remote(ref.at[:, col], kvu.at[side, own_slot], kv_s.at[2 * n + side], kv_r.at[2 * n + side], to)
            )
    for one in kv_copies:
        one.start()
    for one in loads:
        one.wait()
    picker = (
        lax.broadcasted_iota(jnp.int32, (8, 512), 1) // HDIM
        == lax.broadcasted_iota(jnp.int32, (8, 512), 0) - 4
    ).astype(BF)
    for c in range(NZ):
        prod = og[0, :, c * 512 : (c + 1) * 512].astype(F32) * og[1, :, c * 512 : (c + 1) * 512].astype(F32)
        high = prod.astype(BF)
        low = (prod - high.astype(F32)).astype(BF)
        dims = (((1,), (1,)), ((), ()))
        delta = lax.dot_general(picker, high, dims, preferred_element_type=F32)
        delta = delta + lax.dot_general(picker, low, dims, preferred_element_type=F32)
        sbuf[c] = jnp.concatenate([lse_ref[4 * c : 4 * c + 4, :] * LOG2E, delta[4:8]], axis=0)
    for one in keep:
        one.wait()
    for one in kv_copies:
        one.wait_recv()
    mine = pl.ds(pl.multiple_of(y * 8, 8), 8)
    ag_copies = []
    for dy in range(1, NY):
        to = shifted(dy=dy)
        for side in range(2):
            n = (dy - 1) * 2 + side
            ag_copies.append(remote(kvu.at[side, mine], kvu.at[side, mine], ag_s.at[n], ag_r.at[n], to))
    for one in ag_copies:
        one.start()
    halo_copies = []
    for n, step in enumerate((1, -1)):
        to = along(step)
        for side in range(2):
            halo_copies.append(
                remote(
                    kvu.at[side, mine],
                    kvu.at[side, pl.ds(HALO + 8 * n, 8)],
                    hl_s.at[2 * n + side],
                    hl_r.at[2 * n + side],
                    to,
                )
            )
    for one in halo_copies:
        one.start()
    rest = []
    for dz in range(1, NZ):
        to = shifted(dz=dz)
        c = lax.rem(z + dz, NZ)
        n = dz - 1
        rest.append(remote(q_ref.at[:, columns(c, 512)], qb.at[z], q_s.at[2 * n], q_r.at[2 * n], to))
        rest.append(remote(g_ref.at[:, columns(c, 512)], gb.at[z], q_s.at[2 * n + 1], q_r.at[2 * n + 1], to))
        rest.append(remote(sbuf.at[c], stats.at[z], st_s.at[n], st_r.at[n], to))
        rest.append(remote(int_ref, ints.at[z], it_s.at[n], it_r.at[n], to))
    for one in rest:
        one.start()
    own_stats = pltpu.make_async_copy(sbuf.at[z], stats.at[z], local_sem.at[7])
    own_stats.start()
    for one in ag_copies + halo_copies:
        one.wait_recv()
    for g in range(2):
        block = glob_ref[g]
        shard = block // 2
        slot = lax.rem(shard // NI, NY) * 8 + (shard // (NI * NY)) * 2 + lax.rem(block, 2)
        for side in range(2):
            gsend[side, g] = kvu[side, slot]
    gl_copies = []
    for di in range(1, NI):
        gl_copies.append(remote(gsend, grecv.at[di], gl_s.at[di - 1], gl_r.at[di - 1], shifted(di=di)))
    for one in gl_copies:
        one.start()
    grecv[0] = gsend[...]
    for one in gl_copies:
        one.wait_recv()
    for g in range(2):
        holder = lax.rem(glob_ref[g] // 2, NI)
        source = lax.rem(i - holder + NI, NI)
        for side in range(2):
            kvu[side, GLOBAL + g] = grecv[source, side, g]
    for one in kv_copies + ag_copies + halo_copies + gl_copies:
        one.wait_send()
    for one in rest + stay:
        one.wait()
    own_stats.wait()


def compute_kernel(
    glob_ref, ints, qb, gb, kvu, stats,
    dqb, rs, own, dhb, dgl,
    acc,
):
    z, y, i, h = place()
    turn = y * NI + i

    def clear(n, carry):
        acc[0, n] = jnp.zeros((BLOCK, HDIM), F32)
        acc[1, n] = jnp.zeros((BLOCK, HDIM), F32)
        return carry

    lax.fori_loop(0, SLOTS, clear, 0)

    def block_body(n, carry):
        zi = n // 2
        b = lax.rem(n, 2)
        rows = pl.ds(pl.multiple_of(b * BLOCK, BLOCK), BLOCK)
        query = jnp.concatenate([qb[zi, rows, j * HDIM : (j + 1) * HDIM] for j in range(4)], axis=0)
        grad = jnp.concatenate([gb[zi, rows, j * HDIM : (j + 1) * HDIM] for j in range(4)], axis=0)
        tile = stats[zi, :, rows]
        lse = jnp.concatenate([tile[j : j + 1] for j in range(4)], axis=1)
        delta = jnp.concatenate([tile[4 + j : 5 + j] for j in range(4)], axis=1)
        width = ints[zi, 0, 6 + b]
        block_id = (zi * (NY * NI) + turn) * 2 + b
        before = jnp.maximum(zi - (turn == 0).astype(jnp.int32), 0)
        after = jnp.minimum(zi + (turn == NY * NI - 1).astype(jnp.int32), NZ - 1)
        slots = []
        for e in range(5):
            at = b + e - 2
            slot = jnp.where(
                at < 0,
                HALO + before * 2 + at + 2,
                jnp.where(at >= 2, HALO + 8 + after * 2 + at - 2, y * 8 + zi * 2 + at),
            )
            target = block_id + e - 2
            ok = (abs(e - 2) <= width) & (target >= 0) & (target < 2 * NZ * NY * NI)
            slots.append((slot, jnp.where(ok, 0.0, 1e6).astype(F32)))
        for g in range(2):
            slots.append((GLOBAL + g, None))
        for r in range(3):
            block = ints[zi, 0, b * 3 + r]
            shard = block // 2
            slot = lax.rem(shard // NI, NY) * 8 + (shard // (NI * NY)) * 2 + lax.rem(block, 2)
            slots.append((slot, None))
        nt = (((1,), (1,)), ((), ()))
        tn = (((0,), (0,)), ((), ()))
        total = jnp.zeros((HDIM, 512), F32)
        for p in range(5):
            pair = slots[2 * p : 2 * p + 2]
            keys = jnp.concatenate([kvu[0, s] for s, _ in pair], axis=0)
            values = jnp.concatenate([kvu[1, s] for s, _ in pair], axis=0)
            scores = lax.dot_general(keys, query, nt, preferred_element_type=F32) * (SCALE * LOG2E)
            lses = [lse if off is None else lse + off for _, off in pair]
            scores = jnp.concatenate(
                [scores[:BLOCK] - lses[0], scores[BLOCK:] - lses[1]], axis=0
            )
            probs = jnp.exp2(scores)
            prob_grad = lax.dot_general(values, grad, nt, preferred_element_type=F32)
            score_grad = (probs * (prob_grad - delta)).astype(BF)
            value_entry = jnp.dot(probs.astype(BF), grad, preferred_element_type=F32)
            key_entry = jnp.dot(score_grad, query, preferred_element_type=F32)
            total = total + lax.dot_general(keys, score_grad, tn, preferred_element_type=F32)
            for k in range(2):
                s = pair[k][0]
                acc[0, s] += key_entry[k * BLOCK : (k + 1) * BLOCK]
                acc[1, s] += value_entry[k * BLOCK : (k + 1) * BLOCK]
        done = (jnp.transpose(total) * SCALE).astype(BF)
        for j in range(4):
            dqb[zi, rows, j * HDIM : (j + 1) * HDIM] = done[j * BLOCK : (j + 1) * BLOCK]
        return carry

    lax.fori_loop(0, 8, block_body, 0)
    for side in range(2):
        factor = SCALE if side == 0 else 1.0

        def give(n, carry):
            rs[n // 8, side, lax.rem(n, 8)] = (acc[side, n] * factor).astype(BF)
            return carry

        lax.fori_loop(0, 32, give, 0)

        def give_halo(n, carry):
            dhb[n // 8, side, lax.rem(n, 8)] = (acc[side, HALO + n] * factor).astype(BF)
            return carry

        lax.fori_loop(0, 16, give_halo, 0)

        def give_own(n, carry):
            own[side, n] = acc[side, y * 8 + n] * factor
            return carry

        lax.fori_loop(0, 8, give_own, 0)
        for g in range(2):
            dgl[side, g] = (acc[side, GLOBAL + g] * factor).astype(BF)


def return_kernel(
    glob_ref, dqb, rs, own, dhb, dgl,
    dq, dk, dv,
    rsr, hr, g1, g2s, g2r, g3s, g3r, acc, outb,
    local_sem, dq_s, dq_r, rs_s, rs_r, hl_s, hl_r, g1_s, g1_r, g2_s, g2_r, g3_s, g3_r, kv_s, kv_r,
):
    z, y, i, h = place()
    stay = pltpu.make_async_copy(dqb.at[z], dq.at[:, columns(z, 512)], local_sem.at[0])
    stay.start()
    meet()
    g1_copies = []
    for di in range(1, NI):
        part = lax.rem(i + di, NI)
        g1_copies.append(remote(dgl.at[part], g1.at[di], g1_s.at[di - 1], g1_r.at[di - 1], shifted(di=di)))
    rs_copies = []
    for dy in range(1, NY):
        to = lax.rem(y + dy, NY)
        rs_copies.append(remote(rs.at[to], rsr.at[dy - 1], rs_s.at[dy - 1], rs_r.at[dy - 1], shifted(dy=dy)))
    hl_copies = [
        remote(dhb.at[0], hr.at[0], hl_s.at[0], hl_r.at[0], along(-1)),
        remote(dhb.at[1], hr.at[1], hl_s.at[1], hl_r.at[1], along(1)),
    ]
    dq_copies = []
    for dz in range(1, NZ):
        to = lax.rem(z + dz, NZ)
        dq_copies.append(
            remote(dqb.at[to], dq.at[:, columns(z, 512)], dq_s.at[dz - 1], dq_r.at[dz - 1], shifted(dz=dz))
        )
    for one in g1_copies + rs_copies + hl_copies + dq_copies:
        one.start()
    for one in g1_copies:
        one.wait_recv()
    partial = dgl[i].astype(F32)
    for di in range(1, NI):
        partial = partial + g1[di].astype(F32)
    g2s[...] = partial.astype(BF)
    g2_copies = [
        remote(g2s, g2r.at[dy - 1], g2_s.at[dy - 1], g2_r.at[dy - 1], shifted(dy=dy)) for dy in range(1, NY)
    ]
    for one in g2_copies:
        one.start()
    for one in g2_copies:
        one.wait_recv()
    for dy in range(1, NY):
        partial = partial + g2r[dy - 1].astype(F32)
    g3s[...] = partial.astype(BF)
    g3r[i] = g3s[...]
    g3_copies = [
        remote(g3s, g3r.at[i], g3_s.at[di - 1], g3_r.at[di - 1], shifted(di=di)) for di in range(1, NI)
    ]
    for one in g3_copies:
        one.start()
    for one in g3_copies:
        one.wait_recv()
    for one in hl_copies:
        one.wait_recv()
    turn = y * NI + i

    def begin(n, carry):
        zi = n // 2
        b = lax.rem(n, 2)
        block = (zi * (NY * NI) + turn) * 2 + b
        for side in range(2):
            total = own[side, n]
            total = total + hr[0, side, n].astype(F32) + hr[1, side, n].astype(F32)
            for g in range(2):
                hit = (jnp.zeros((BLOCK, HDIM), jnp.int32) + glob_ref[g]) == block
                both = jnp.concatenate([g3r[2 * side, g], g3r[2 * side + 1, g]], axis=0).astype(F32)
                total = total + jnp.where(hit, both, 0.0)
            acc[side, n] = total
        return carry

    lax.fori_loop(0, 8, begin, 0)
    for one in rs_copies:
        one.wait_recv()

    def finish(n, carry):
        for side in range(2):
            total = acc[side, n]
            for dy in range(NY - 1):
                total = total + rsr[dy, side, n].astype(F32)
            outb[side, n] = total.astype(BF)
        return carry

    lax.fori_loop(0, 8, finish, 0)
    col = columns(h * NZ + z, HDIM)
    mine = z * 2 + h
    home = [
        pltpu.make_async_copy(outb.at[0, mine], dk.at[:, col], local_sem.at[1]),
        pltpu.make_async_copy(outb.at[1, mine], dv.at[:, col], local_sem.at[2]),
    ]
    for one in home:
        one.start()
    kv_copies = []
    for n, (dz, dh) in enumerate(ZH):
        to = shifted(dz=dz, dh=dh)
        slot = lax.rem(z + dz, NZ) * 2 + lax.rem(h + dh, 2)
        for side, ref in enumerate((dk, dv)):
            kv_copies.append(
                remote(outb.at[side, slot], ref.at[:, col], kv_s.at[2 * n + side], kv_r.at[2 * n + side], to)
            )
    for one in kv_copies:
        one.start()
    for one in home + [stay] + kv_copies + dq_copies:
        one.wait()
    for one in g1_copies + rs_copies + hl_copies + g2_copies + g3_copies:
        one.wait_send()


ANY = pl.BlockSpec(memory_space=pl.ANY)
VMEM = pl.BlockSpec(memory_space=pltpu.VMEM)
SMEM = pl.BlockSpec(memory_space=pltpu.SMEM)
DMA = pltpu.SemaphoreType.DMA


def params(collective_id=None):
    if collective_id is None:
        return pltpu.CompilerParams(vmem_limit_bytes=40 * 2**20)
    return pltpu.CompilerParams(
        collective_id=collective_id, has_side_effects=True, vmem_limit_bytes=40 * 2**20
    )


def on_device(
    queries, key_heads, value_heads, output, output_grad, log_totals, random_blocks, window_width, global_blocks
):
    row = jnp.pad(jnp.concatenate([random_blocks.reshape(-1), window_width]), (0, 120))
    listed = jnp.broadcast_to(row[None], (8, 128))
    shape = jax.ShapeDtypeStruct
    qb, gb, kvu, stats, ints = pl.pallas_call(
        gather_kernel,
        out_shape=(
            shape((NZ, 256, 512), BF),
            shape((NZ, 256, 512), BF),
            shape((2, SLOTS, BLOCK, HDIM), BF),
            shape((NZ, 8, 256), F32),
            shape((NZ, 8, 128), jnp.int32),
        ),
        in_specs=[SMEM, ANY, ANY, ANY, ANY, ANY, VMEM, ANY],
        out_specs=(ANY, ANY, VMEM, VMEM, ANY),
        scratch_shapes=[
            pltpu.VMEM((2, 256, 2048), BF),
            pltpu.VMEM((NZ, 8, 256), F32),
            pltpu.VMEM((2, 2, BLOCK, HDIM), BF),
            pltpu.VMEM((NI, 2, 2, BLOCK, HDIM), BF),
            DMA((8,)),
            DMA((14,)), DMA((14,)),
            DMA((6,)), DMA((6,)),
            DMA((3,)), DMA((3,)),
            DMA((3,)), DMA((3,)),
            DMA((6,)), DMA((6,)),
            DMA((4,)), DMA((4,)),
            DMA((3,)), DMA((3,)),
        ],
        compiler_params=params(0),
        name="gather",
    )(global_blocks, queries, key_heads, value_heads, output, output_grad, log_totals, listed)
    dqb, rs, own, dhb, dgl = pl.pallas_call(
        compute_kernel,
        out_shape=(
            shape((NZ, 256, 512), BF),
            shape((NY, 2, 8, BLOCK, HDIM), BF),
            shape((2, 8, BLOCK, HDIM), F32),
            shape((2, 2, 8, BLOCK, HDIM), BF),
            shape((2, 2, BLOCK, HDIM), BF),
        ),
        in_specs=[SMEM, SMEM, VMEM, VMEM, VMEM, VMEM],
        out_specs=(VMEM,) * 5,
        scratch_shapes=[pltpu.VMEM((2, SLOTS, BLOCK, HDIM), F32)],
        compiler_params=params(),
        name="compute",
    )(global_blocks, ints, qb, gb, kvu, stats)
    parts = jnp.transpose(dgl.reshape(2, 2, 2, 64, HDIM), (0, 2, 1, 3, 4)).reshape(4, 2, 64, HDIM)
    return pl.pallas_call(
        return_kernel,
        out_shape=(
            shape((256, 2048), BF),
            shape((BLOCK, 1024), BF),
            shape((BLOCK, 1024), BF),
        ),
        in_specs=[SMEM, ANY, ANY, VMEM, ANY, VMEM],
        out_specs=(ANY, ANY, ANY),
        scratch_shapes=[
            pltpu.VMEM((NY - 1, 2, 8, BLOCK, HDIM), BF),
            pltpu.VMEM((2, 2, 8, BLOCK, HDIM), BF),
            pltpu.VMEM((NI, 2, 64, HDIM), BF),
            pltpu.VMEM((2, 64, HDIM), BF),
            pltpu.VMEM((NY - 1, 2, 64, HDIM), BF),
            pltpu.VMEM((2, 64, HDIM), BF),
            pltpu.VMEM((NI, 2, 64, HDIM), BF),
            pltpu.VMEM((2, 8, BLOCK, HDIM), F32),
            pltpu.VMEM((2, 8, BLOCK, HDIM), BF),
            DMA((3,)),
            DMA((3,)), DMA((3,)),
            DMA((3,)), DMA((3,)),
            DMA((2,)), DMA((2,)),
            DMA((3,)), DMA((3,)),
            DMA((3,)), DMA((3,)),
            DMA((3,)), DMA((3,)),
            DMA((14,)), DMA((14,)),
        ],
        compiler_params=params(1),
        name="give_back",
    )(global_blocks, dqb, rs, own, dhb, parts)


def solution(mesh):
    placed = (
        P(("outer", "inner"), "head"),
        P(("outer", "inner", "head"), None),
        P(("outer", "inner", "head"), None),
        P(("outer", "inner"), "head"),
        P(("outer", "inner"), "head"),
        P("head", ("outer", "inner")),
        P(("outer", "inner"), None),
        P(("outer", "inner")),
        P(),
    )
    return jax.shard_map(
        on_device,
        mesh=mesh,
        in_specs=placed,
        out_specs=(
            P(("outer", "inner"), "head"),
            P(("outer", "inner", "head"), None),
            P(("outer", "inner", "head"), None),
        ),
        check_vma=False,
    )
```

time: 1280 us -> 130 us (0.10)
  waiting for transfers between devices: 1040 us -> 0 us
  Pallas kernels: 0 us -> 117 us
  local copies, waits for them, and re-layouts: 104 us -> 10.1 us
  matrix products: 41.9 us -> 0 us
  starting transfers between devices: 41.6 us -> 0 us
  other arithmetic: 21.8 us -> 0.74 us
  between operations: 21.5 us -> 0.68 us
    psum x2 -> x0, waiting for transfers between devices: 1020 us -> none  [the longest x1 511 us: from_root(): return lax.psum(jnp.where(mine, value, jnp.zeros_like(value)), axis)]
    pallas_call x0 -> x3, Pallas kernels: none -> 117 us  [the longest x1 50.3 us: on_device(): pl.pallas_call(gather_kernel, out_shape=(shape((NZ, 256, 512), BF), shape...]
    dot_general x21 -> x0, matrix products: 41.9 us -> none  [the longest x4 10.7 us: on_device(): jnp.einsum('bgqjk,bjkd->bqgd', score_grad, key_tiles, preferred_element_t...]
    reshape x20 -> x1, local copies, waits for them, and re-layouts: 37.1 us -> 0.76 us  [on_device(): random_blocks.reshape(-1)]
    all_to_all x5 -> x0, starting transfers between devices: 29.9 us -> none  [the longest x1 9.86 us: on_device(): lax.all_to_all(slots_out.reshape(2, outer_size, slot_cap, BLOCK, kv_width...]
    all_to_all x6 -> x0, local copies, waits for them, and re-layouts: 14.8 us -> none  [the longest x1 10.1 us: on_device(): lax.all_to_all(slots_out.reshape(2, outer_size, slot_cap, BLOCK, kv_width...]
  transfers between devices with their start and end apart: 12 -> 0, of which waited for: 7 -> 0; matrix products, arithmetic and copies ran while one was open for 9% -> 0% of each run, Pallas kernels for 0% -> 0%
where the time goes in v1:
time: 130 us; the launch traced here: 129 us
  Pallas kernels  117 us (90%)
  local copies, waits for them, and re-layouts  10.1 us (8%)
    pallas_call x1, Pallas kernels, on_device(): pl.pallas_call(gather_kernel, out_shape=(shape((NZ, 256, 512), BF), shape...  50.3 us
    pallas_call x1, Pallas kernels, on_device(): pl.pallas_call(return_kernel, out_shape=(shape((256, 2048), BF), shape((B...  49.7 us
    pallas_call x1, Pallas kernels, on_device(): pl.pallas_call(compute_kernel, out_shape=(shape((NZ, 256, 512), BF), shap...  17.3 us
    unnamed x17, local copies, waits for them, and re-layouts  9.32 us

profile of v1, /device:TPU:8, one launch (start us, length us, event | category | flops | bytes accessed | tf_op | source)
XLA Modules:
  0.0 128.8 jit_solution(433252683139156180)
XLA Ops:
  0.6 0.8 reshape.14
  1.4 0.7 pad_add_fusion
  2.1 0.0 copy-start
  2.1 1.2 copy-done
  3.4 0.0 copy-start.1
  3.4 1.2 copy-done.1
  4.6 0.0 copy-start.2
  4.6 1.2 copy-done.2
  5.8 0.0 copy-start.3
  5.8 0.9 copy-done.3
  6.8 0.0 copy-start.4
  6.8 0.9 copy-done.4
  7.7 0.0 copy-start.5
  7.7 0.7 copy-done.5
  8.4 0.0 copy-start.6
  8.4 0.7 copy-done.6
  9.1 50.3 %gather.1 = (bf16[4,256,512]{2,1,0:T(8,128)(2,1)S(1)}, bf16[4,256,512]{2,1,0:T(8,128)(2,1)S(1)}, bf16[2,50,128,128]{3,2,1,0:T(8,128)(2,1)S(1)}, f32[4,8,256]{2,1,0:T(8,128)S(1)}, s32[4,8,128]{2,1,0:T(8,128)S(1)}) custom-call(s32[2]{0:T(128)S(1)} %copy-done.6, bf16[256,2048]{1,0:T(8,128)(2,1)S(1)} %copy-done, bf16[128,1024]{1,0:T(8,128)(2,1)S(1)} %copy-done.3, ...), custom_call_target="tpu_custom_call" | custom-call | tf_op jit(solution)/shard_map/gather/pallas_call | solution.py:417
  59.4 17.3 %compute.1 = (bf16[4,256,512]{2,1,0:T(8,128)(2,1)S(1)}, bf16[4,2,8,128,128]{4,3,2,1,0:T(8,128)(2,1)S(1)}, f32[2,8,128,128]{3,2,1,0:T(8,128)S(1)}, bf16[2,2,8,128...) custom-call(s32[2]{0:T(128)S(1)} %copy-done.6, s32[4,8,128]{2,1,0:T(8,128)S(1)} %get-tuple-element.13.ints, ...), custom_call_target="tpu_custom_call" | custom-call | tf_op jit(solution)/shard_map/compute/pallas_call | solution.py:445
  76.7 49.7 %give_back.1 = (bf16[256,2048]{1,0:T(8,128)(2,1)S(1)}, bf16[128,1024]{1,0:T(8,128)(2,1)S(1)}, bf16[128,1024]{1,0:T(8,128)(2,1)S(1)}) custom-call(s32[2]{0:T(128)S(1)} %copy-done.6, bf16[4,256,512]{2,1,0:T(8,128)(2,1)S(1)} %get-tuple-element.18.dqb, bf16[4,2,8,128,128]{4,3,2,1,0:T(8,128)(2,1)S(1)} %get-tuple-element.19.rs, ...), custom_call_target="tpu_custom_call" | custom-call | tf_op jit(solution)/shard_map/give_back/pallas_call | solution.py:461
  126.4 1.0 copy.15
  127.4 0.7 copy.16
  128.1 0.7 copy.17
  (4 shorter events, 0.0 us)
Async XLA Ops:
  2.1 1.2 copy-start
  3.4 1.2 copy-start.1
  4.6 1.2 copy-start.2
  5.8 0.9 copy-start.3
  6.8 0.9 copy-start.4
  7.7 0.7 copy-start.5
  8.4 0.7 copy-start.6

commit v2 on v0

v2 whole, which is shorter than its diff:
```python
import math

import jax
import jax.numpy as jnp
from jax import lax
from jax.experimental import pallas as pl
from jax.experimental.pallas import tpu as pltpu
from jax.sharding import PartitionSpec as P

MESH = pl.DeviceIdType.MESH
HDIM = 128
BLOCK = 128
N = 4
SCALE = HDIM ** (-0.5)
LOG2E = math.log2(math.e)
YH = [(dy, dh) for dy in range(4) for dh in range(2) if (dy, dh) != (0, 0)]
BF = jnp.bfloat16
F32 = jnp.float32
I32 = jnp.int32
NT = (((1,), (1,)), ((), ()))
TN = (((0,), (0,)), ((), ()))


def place():
    outer = lax.axis_index("outer")
    return outer // N, lax.rem(outer, N), lax.axis_index("inner"), lax.axis_index("head")


def device(z, y, i, h):
    return (z * N + y, i, h)


def shifted(dz=0, dy=0, di=0, dh=0):
    z, y, i, h = place()
    return device(lax.rem(z + dz, N), lax.rem(y + dy, N), lax.rem(i + di, N), lax.rem(h + dh, 2))


def following(shard):
    z, y, i, h = place()
    wrap = (i == N - 1).astype(I32)
    spot = lax.rem(shard + wrap, N)
    cross = wrap * jnp.where(shard == N - 1, 1, 0)
    return device(lax.rem(z + cross, N), y, lax.rem(i + 1, N), h), spot


def preceding(shard):
    z, y, i, h = place()
    wrap = (i == 0).astype(I32)
    spot = lax.rem(shard - wrap + N, N)
    cross = wrap * jnp.where(shard == 0, 1, 0)
    return device(lax.rem(z - cross + N, N), y, lax.rem(i + N - 1, N), h), spot


def meet():
    barrier = pltpu.get_barrier_semaphore()
    found = [shifted(dy=dy, dh=dh) for dy, dh in YH]
    found += [shifted(dz=dz) for dz in range(1, N)]
    found += [shifted(di=di) for di in range(1, N)]
    found += [following(N - 1)[0], preceding(0)[0]]
    for one in found:
        pl.semaphore_signal(barrier, inc=1, device_id=one, device_id_type=MESH)
    pl.semaphore_wait(barrier, len(found))


def remote(src, dst, send, recv, to):
    return pltpu.make_async_remote_copy(
        src_ref=src, dst_ref=dst, send_sem=send, recv_sem=recv, device_id=to, device_id_type=MESH
    )


def columns(index, width):
    return pl.ds(pl.multiple_of(index * width, width), width)


def offset_of(k):
    if isinstance(k, int):
        return (0, 1, 3, 2)[k]
    return k + (k == 2).astype(I32) - (k == 3).astype(I32)


def block_slot(block):
    shard = block // 2
    return (shard // (N * N)) * 8 + lax.rem(shard // N, N) * 2 + lax.rem(block, 2)


def fused(
    glob_ref, rand_ref, width_ref, q_ref, k_ref, v_ref, o_ref, g_ref, lse_ref,
    dq, dk, dv,
    og, lseb, sbuf, intb, intr, ints, stats, qb, gb, kvu, hal, gsend, grecv,
    dqt, acc, dhb, hrn, hrp, ent, spots, rsb, rsr, gacc, dglb, g1r, g2s, g2r, g3r, dqb, outb,
    loc, kv_s, kv_r, q_s, q_r, st_s, st_r, it_s, it_r, ag_s, ag_r, hn_s, hn_r, hp_s, hp_r, gl_s, gl_r,
    dn_s, dn_r, dp_s, dp_r, rs_s, rs_r, g1_s, g1_r, g2_s, g2_r, g3_s, g3_r, dq_s, dq_r, out_s, out_r,
):
    z, y, i, h = place()
    own_slot = z * 8 + y * 2 + h
    own_col = columns(h * N + y, HDIM)
    loads = [
        pltpu.make_async_copy(o_ref, og.at[0], loc.at[0]),
        pltpu.make_async_copy(g_ref, og.at[1], loc.at[1]),
        pltpu.make_async_copy(lse_ref, lseb, loc.at[2]),
    ]
    keep = [
        pltpu.make_async_copy(k_ref.at[:, own_col], kvu.at[own_slot, 0], loc.at[3]),
        pltpu.make_async_copy(v_ref.at[:, own_col], kvu.at[own_slot, 1], loc.at[4]),
    ]
    stay = [
        pltpu.make_async_copy(q_ref.at[:, columns(y, 512)], qb.at[y], loc.at[5]),
        pltpu.make_async_copy(g_ref.at[:, columns(y, 512)], gb.at[y], loc.at[6]),
    ]
    for one in keep + loads + stay:
        one.start()
    lane = lax.broadcasted_iota(I32, (8, 128), 1)
    row = jnp.zeros((8, 128), I32)
    for b in range(2):
        for r in range(3):
            row = jnp.where(lane == b * 3 + r, rand_ref[b, r], row)
        row = jnp.where(lane == 6 + b, width_ref[b], row)
    intb[...] = row
    meet()

    it_copies = [
        remote(intb, intr.at[y], it_s.at[dy - 1], it_r.at[dy - 1], shifted(dy=dy)) for dy in range(1, N)
    ]
    kv_copies = {}
    for n, (dy, dh) in enumerate(YH):
        to = shifted(dy=dy, dh=dh)
        col = columns(lax.rem(h + dh, 2) * N + lax.rem(y + dy, N), HDIM)
        for side, ref in enumerate((k_ref, v_ref)):
            kv_copies[dy, dh, side] = remote(
                ref.at[:, col], kvu.at[own_slot, side], kv_s.at[2 * n + side], kv_r.at[2 * n + side], to
            )
    for key in sorted(kv_copies, key=lambda s: ((0, 1, 3, 2)[s[0]], s[1], s[2])):
        kv_copies[key].start()
    for one in it_copies:
        one.start()
    intr[y] = row

    for one in loads:
        one.wait()
    picker = (
        lax.broadcasted_iota(I32, (8, 512), 1) // HDIM == lax.broadcasted_iota(I32, (8, 512), 0) - 4
    ).astype(BF)
    for c in range(N):
        prod = og[0, :, c * 512 : (c + 1) * 512].astype(F32) * og[1, :, c * 512 : (c + 1) * 512].astype(F32)
        high = prod.astype(BF)
        low = (prod - high.astype(F32)).astype(BF)
        delta = lax.dot_general(picker, high, NT, preferred_element_type=F32)
        delta = delta + lax.dot_general(picker, low, NT, preferred_element_type=F32)
        sbuf[c] = jnp.concatenate([lseb[4 * c : 4 * c + 4, :] * LOG2E, delta[4:8]], axis=0)
    st_copies = [
        remote(sbuf.at[lax.rem(y + dy, N)], stats.at[y], st_s.at[dy - 1], st_r.at[dy - 1], shifted(dy=dy))
        for dy in range(1, N)
    ]
    for one in st_copies:
        one.start()
    own_stats = pltpu.make_async_copy(sbuf.at[y], stats.at[y], loc.at[7])
    own_stats.start()
    for one in keep:
        one.wait()

    ag_copies, hn_copies, hp_copies = [], [], []
    for dy in (0, 1, 3, 2):
        shard = lax.rem(y - dy + N, N)
        for dh in range(2):
            for side in range(2):
                if (dy, dh) != (0, 0):
                    kv_copies[dy, dh, side].wait_recv()
        here = pl.ds(pl.multiple_of(z * 8 + shard * 2, 2), 2)
        for dz in range(1, N):
            n = dy * 3 + dz - 1
            ag_copies.append(remote(kvu.at[here], kvu.at[here], ag_s.at[n], ag_r.at[n], shifted(dz=dz)))
            ag_copies[-1].start()
        to, spot = following(shard)
        hn_copies.append(remote(kvu.at[here], hal.at[0, spot], hn_s.at[dy], hn_r.at[spot], to))
        hn_copies[-1].start()
        to, spot = preceding(shard)
        hp_copies.append(remote(kvu.at[here], hal.at[1, spot], hp_s.at[dy], hp_r.at[spot], to))
        hp_copies[-1].start()
    q_copies = {}
    for dy in (1, 3, 2):
        c = lax.rem(y + dy, N)
        for side, (ref, dst) in enumerate(((q_ref, qb), (g_ref, gb))):
            n = 2 * (dy - 1) + side
            q_copies[dy, side] = remote(
                ref.at[:, columns(c, 512)], dst.at[y], q_s.at[n], q_r.at[n], shifted(dy=dy)
            )
            q_copies[dy, side].start()

    for one in it_copies + st_copies:
        one.wait_recv()
    own_stats.wait()
    to_scalar = pltpu.make_async_copy(intr, ints, loc.at[8])
    to_scalar.start()
    to_scalar.wait()
    for shard in range(N):
        ent[shard, 0] = jnp.zeros((2, BLOCK, HDIM), BF)
    for b in range(2):
        dqt[6 + b] = jnp.zeros((HDIM, 512), F32)
    for g in range(2):
        for side in range(2):
            gacc[g, side] = jnp.zeros((BLOCK, HDIM), F32)

    def find(slot, carry):
        for shard in range(N):
            spot = 0
            for r in range(6):
                spot = jnp.where(block_slot(ints[shard, 0, r]) == slot, r + 1, spot)
            spots[slot, shard] = spot
        return carry

    lax.fori_loop(0, 32, find, 0)

    def load_block(shard, b):
        rows = slice(b * BLOCK, (b + 1) * BLOCK)
        query = jnp.concatenate([qb[shard, rows, j * HDIM : (j + 1) * HDIM] for j in range(4)], axis=0)
        grad = jnp.concatenate([gb[shard, rows, j * HDIM : (j + 1) * HDIM] for j in range(4)], axis=0)
        tile = stats[shard, :, rows]
        lse = jnp.concatenate([tile[j : j + 1] for j in range(4)], axis=1)
        delta = jnp.concatenate([tile[4 + j : 5 + j] for j in range(4)], axis=1)
        return query, grad, lse, delta

    def attend(pairs, lses, query, grad, delta):
        count = len(pairs)
        keys = jnp.concatenate([k for k, _ in pairs], axis=0)
        values = jnp.concatenate([v for _, v in pairs], axis=0)
        scores = lax.dot_general(keys, query, NT, preferred_element_type=F32) * (SCALE * LOG2E)
        scores = jnp.concatenate([scores[k * BLOCK : (k + 1) * BLOCK] - lses[k] for k in range(count)], axis=0)
        probs = jnp.exp2(scores)
        prob_grad = lax.dot_general(values, grad, NT, preferred_element_type=F32)
        score_grad = (probs * (prob_grad - delta)).astype(BF)
        value_entry = jnp.dot(probs.astype(BF), grad, preferred_element_type=F32)
        key_entry = jnp.dot(score_grad, query, preferred_element_type=F32)
        turned = lax.dot_general(keys, score_grad, TN, preferred_element_type=F32)
        cut = [slice(k * BLOCK, (k + 1) * BLOCK) for k in range(count)]
        return [key_entry[c] for c in cut], [value_entry[c] for c in cut], turned

    def window(k, add):
        shard = lax.rem(y - offset_of(k) + N, N)
        for b in range(2):
            query, grad, lse, delta = load_block(shard, b)
            width = ints[shard, 0, 6 + b]
            block_id = ((z * N + shard) * N + i) * 2 + b
            total = None
            for group in ((0, 1), (2, 3), (4,)):
                pairs, lses = [], []
                for e in group:
                    at = b + e - 2
                    if at < 0:
                        pairs.append((hal[0, shard, at + 2, 0], hal[0, shard, at + 2, 1]))
                    elif at >= 2:
                        pairs.append((hal[1, shard, at - 2, 0], hal[1, shard, at - 2, 1]))
                    else:
                        slot = z * 8 + shard * 2 + at
                        pairs.append((kvu[slot, 0], kvu[slot, 1]))
                    target = block_id + e - 2
                    ok = (abs(e - 2) <= width) & (target >= 0) & (target < 128)
                    lses.append(lse + jnp.where(ok, 0.0, 1e6).astype(F32))
                dks, dvs, turned = attend(pairs, lses, query, grad, delta)
                total = turned if total is None else total + turned
                for e, dk_e, dv_e in zip(group, dks, dvs):
                    at = b + e
                    if b == 0 or at == 5:
                        acc[shard, at, 0] = dk_e
                        acc[shard, at, 1] = dv_e
                    else:
                        acc[shard, at, 0] += dk_e
                        acc[shard, at, 1] += dv_e
            if add:
                dqt[2 * k + b] += total
            else:
                dqt[2 * k + b] = total
        for n, start in enumerate((0, 4)):
            for b in range(2):
                dhb[n, shard, b, 0] = (acc[shard, start + b, 0] * SCALE).astype(BF)
                dhb[n, shard, b, 1] = acc[shard, start + b, 1].astype(BF)
        to, spot = preceding(shard)
        remote(dhb.at[0, shard], hrn.at[spot], dn_s.at[shard], dn_r.at[spot], to).start()
        to, spot = following(shard)
        remote(dhb.at[1, shard], hrp.at[spot], dp_s.at[shard], dp_r.at[spot], to).start()

    def wait_queries(k):
        dy = offset_of(k)
        for side, (ref, dst) in enumerate(((q_ref, qb), (g_ref, gb))):
            n = 2 * (dy - 1) + side
            remote(
                ref.at[:, columns(y, 512)], dst.at[y], q_s.at[n], q_r.at[n], shifted(dy=1)
            ).wait_recv()

    for one in stay:
        one.wait()
    for shard in range(N):
        remote(hal.at[0, shard], hal.at[0, shard], hn_s.at[shard], hn_r.at[shard], shifted(di=1)).wait_recv()
        remote(hal.at[1, shard], hal.at[1, shard], hp_s.at[shard], hp_r.at[shard], shifted(di=1)).wait_recv()

    def early(k, carry):
        @pl.when(k > 0)
        def _():
            wait_queries(k)

        window(k, False)
        return carry

    lax.fori_loop(0, 3, early, 0)

    for one in ag_copies:
        one.wait_recv()
    for g in range(2):
        gsend[g] = kvu[block_slot(glob_ref[g])]
    gl_copies = [
        remote(gsend, grecv.at[di], gl_s.at[di - 1], gl_r.at[di - 1], shifted(di=di)) for di in range(1, N)
    ]
    for one in gl_copies:
        one.start()
    grecv[0] = gsend[...]

    def random(k, carry):
        @pl.when(k == 3)
        def _():
            wait_queries(k)

        shard = lax.rem(y - offset_of(k) + N, N)
        for b in range(2):
            query, grad, lse, delta = load_block(shard, b)
            total = None
            for group in ((0, 1), (2,)):
                slots = [block_slot(ints[shard, 0, b * 3 + r]) for r in group]
                pairs = [(kvu[s, 0], kvu[s, 1]) for s in slots]
                dks, dvs, turned = attend(pairs, [lse] * len(group), query, grad, delta)
                total = turned if total is None else total + turned
                for r, dk_e, dv_e in zip(group, dks, dvs):
                    ent[shard, 1 + b * 3 + r, 0] = (dk_e * SCALE).astype(BF)
                    ent[shard, 1 + b * 3 + r, 1] = dv_e.astype(BF)
            dqt[2 * k + b] += total
        return carry

    lax.fori_loop(0, N, random, 0)

    def named(slot):
        total = None
        for shard in range(N):
            one = ent[shard, spots[slot, shard]].astype(F32)
            total = one if total is None else total + one
        return total

    rs_copies = []
    for dy in range(N):
        shard = lax.rem(y + dy, N)
        for dz in range(1, N):
            to = lax.rem(z + dz, N)

            def fill(b, carry, to=to, shard=shard, dz=dz):
                rsb[dz - 1, shard, b] = named(to * 8 + shard * 2 + b).astype(BF)
                return carry

            lax.fori_loop(0, 2, fill, 0)
            n = dy * 3 + dz - 1
            rs_copies.append(
                remote(rsb.at[dz - 1, shard], rsr.at[dz - 1, shard], rs_s.at[n], rs_r.at[n], shifted(dz=dz))
            )
            rs_copies[-1].start()

    for one in gl_copies:
        one.wait_recv()
    globe = []
    for g in range(2):
        source = lax.rem(i - lax.rem(glob_ref[g] // 2, N) + N, N)
        globe.append(source)

    def dq_copy(k):
        dy = offset_of(k)
        shard = lax.rem(y - dy + N, N)
        return remote(
            dqb.at[shard], dq.at[:, columns(y, 512)], dq_s.at[dy - 1], dq_r.at[dy - 1], device(z, shard, i, h)
        )

    dq_home = pltpu.make_async_copy(dqb.at[y], dq.at[:, columns(y, 512)], loc.at[9])

    def whole(k, carry):
        shard = lax.rem(y - offset_of(k) + N, N)
        for b in range(2):
            query, grad, lse, delta = load_block(shard, b)
            pairs = [(grecv[globe[g], g, 0], grecv[globe[g], g, 1]) for g in range(2)]
            dks, dvs, turned = attend(pairs, [lse] * 2, query, grad, delta)
            for g in range(2):
                gacc[g, 0] += dks[g]
                gacc[g, 1] += dvs[g]
            done = (jnp.transpose(dqt[2 * k + b] + turned) * SCALE).astype(BF)
            for j in range(4):
                dqb[shard, b * BLOCK : (b + 1) * BLOCK, j * HDIM : (j + 1) * HDIM] = done[
                    j * BLOCK : (j + 1) * BLOCK
                ]

        @pl.when(k == 0)
        def _():
            dq_home.start()

        @pl.when(k > 0)
        def _():
            dq_copy(k).start()

        return carry

    def late(k, carry):
        window(k, True)
        return carry

    lax.fori_loop(3, 4, late, 0)
    lax.fori_loop(0, N, whole, 0)

    for g in range(2):
        dglb[2 * g] = (gacc[g, 0] * SCALE).astype(BF)
        dglb[2 * g + 1] = gacc[g, 1].astype(BF)
    g1_copies = [
        remote(dglb.at[lax.rem(i + di, N)], g1r.at[di - 1], g1_s.at[di - 1], g1_r.at[di - 1], shifted(di=di))
        for di in range(1, N)
    ]
    for one in g1_copies:
        one.start()
    for one in g1_copies:
        one.wait_recv()
    partial = dglb[i].astype(F32)
    for n in range(3):
        partial = partial + g1r[n].astype(F32)
    g2s[0] = partial.astype(BF)
    g2_copies = [
        remote(g2s.at[0], g2r.at[dz - 1], g2_s.at[dz - 1], g2_r.at[dz - 1], shifted(dz=dz)) for dz in range(1, N)
    ]
    for one in g2_copies:
        one.start()
    for one in g2_copies:
        one.wait_recv()
    for n in range(3):
        partial = partial + g2r[n].astype(F32)
    g2s[1] = partial.astype(BF)
    g3r[i] = g2s[1]
    g3_copies = [
        remote(g2s.at[1], g3r.at[i], g3_s.at[di - 1], g3_r.at[di - 1], shifted(di=di)) for di in range(1, N)
    ]
    for one in g3_copies:
        one.start()
    for one in g3_copies:
        one.wait_recv()
    for shard in range(N):
        remote(dhb.at[0, shard], hrn.at[shard], dn_s.at[shard], dn_r.at[shard], shifted(di=1)).wait_recv()
        remote(dhb.at[1, shard], hrp.at[shard], dp_s.at[shard], dp_r.at[shard], shifted(di=1)).wait_recv()

    out_copies, home = [], []
    for dy in range(N):
        shard = lax.rem(y + dy, N)
        for dz in range(1, N):
            rs_copies[dy * 3 + dz - 1].wait_recv()

        def close(b, carry, shard=shard):
            block_id = ((z * N + shard) * N + i) * 2 + b
            extra = named(z * 8 + shard * 2 + b)
            for side in range(2):
                total = acc[shard, 2 + b, side] * (SCALE if side == 0 else 1.0) + extra[side]
                total = total + hrn[shard, b, side].astype(F32) + hrp[shard, b, side].astype(F32)
                for n in range(3):
                    total = total + rsr[n, shard, b, side].astype(F32)
                for g in range(2):
                    hit = (jnp.zeros((BLOCK, HDIM), I32) + glob_ref[g]) == block_id
                    total = total + jnp.where(hit, g3r[2 * g + side].astype(F32), 0.0)
                outb[shard, b, side] = total.astype(BF)
            return carry

        lax.fori_loop(0, 2, close, 0)
        for dh in range(2):
            b = lax.rem(h + dh, 2)
            for side, ref in enumerate((dk, dv)):
                if (dy, dh) == (0, 0):
                    home.append(
                        pltpu.make_async_copy(outb.at[shard, b, side], ref.at[:, own_col], loc.at[10 + side])
                    )
                    home[-1].start()
                else:
                    n = 2 * YH.index((dy, dh)) + side
                    out_copies.append(
                        remote(
                            outb.at[shard, b, side],
                            ref.at[:, own_col],
                            out_s.at[n],
                            out_r.at[n],
                            shifted(dy=dy, dh=dh),
                        )
                    )
                    out_copies[-1].start()
    for one in out_copies + home + [dq_home]:
        one.wait()
    for k in range(1, N):
        dq_copy(k).wait()
    for one in list(kv_copies.values()) + list(q_copies.values()) + it_copies + st_copies:
        one.wait_send()
    for one in ag_copies + hn_copies + hp_copies + gl_copies + rs_copies + g1_copies + g2_copies + g3_copies:
        one.wait_send()
    for shard in range(N):
        remote(dhb.at[0, shard], hrn.at[shard], dn_s.at[shard], dn_r.at[shard], shifted(di=1)).wait_send()
        remote(dhb.at[1, shard], hrp.at[shard], dp_s.at[shard], dp_r.at[shard], shifted(di=1)).wait_send()


HBM = pl.BlockSpec(memory_space=pltpu.HBM)
SMEM = pl.BlockSpec(memory_space=pltpu.SMEM)
DMA = pltpu.SemaphoreType.DMA


def on_device(
    queries, key_heads, value_heads, output, output_grad, log_totals, random_blocks, window_width, global_blocks
):
    shape = jax.ShapeDtypeStruct
    tile = (BLOCK, HDIM)
    twice = lambda n: [DMA((n,)), DMA((n,))]
    return pl.pallas_call(
        fused,
        out_shape=(
            shape((256, 2048), BF),
            shape((BLOCK, 1024), BF),
            shape((BLOCK, 1024), BF),
        ),
        in_specs=[SMEM, SMEM, SMEM] + [HBM] * 6,
        out_specs=(HBM, HBM, HBM),
        scratch_shapes=[
            pltpu.VMEM((2, 256, 2048), BF),
            pltpu.VMEM((16, 256), F32),
            pltpu.VMEM((N, 8, 256), F32),
            pltpu.VMEM((8, 128), I32),
            pltpu.VMEM((N, 8, 128), I32),
            pltpu.SMEM((N, 8, 128), I32),
            pltpu.VMEM((N, 8, 256), F32),
            pltpu.VMEM((N, 256, 512), BF),
            pltpu.VMEM((N, 256, 512), BF),
            pltpu.VMEM((32, 2) + tile, BF),
            pltpu.VMEM((2, N, 2, 2) + tile, BF),
            pltpu.VMEM((2, 2) + tile, BF),
            pltpu.VMEM((N, 2, 2) + tile, BF),
            pltpu.VMEM((8, HDIM, 512), F32),
            pltpu.VMEM((N, 6, 2) + tile, F32),
            pltpu.VMEM((2, N, 2, 2) + tile, BF),
            pltpu.VMEM((N, 2, 2) + tile, BF),
            pltpu.VMEM((N, 2, 2) + tile, BF),
            pltpu.VMEM((N, 7, 2) + tile, BF),
            pltpu.SMEM((32, N), I32),
            pltpu.VMEM((3, N, 2, 2) + tile, BF),
            pltpu.VMEM((3, N, 2, 2) + tile, BF),
            pltpu.VMEM((2, 2) + tile, F32),
            pltpu.VMEM((4,) + tile, BF),
            pltpu.VMEM((3,) + tile, BF),
            pltpu.VMEM((2,) + tile, BF),
            pltpu.VMEM((3,) + tile, BF),
            pltpu.VMEM((4,) + tile, BF),
            pltpu.VMEM((N, 256, 512), BF),
            pltpu.VMEM((N, 2, 2) + tile, BF),
            DMA((12,)),
        ]
        + twice(14) + twice(6) + twice(3) + twice(3) + twice(12) + twice(4) + twice(4) + twice(3)
        + twice(4) + twice(4) + twice(12) + twice(3) + twice(3) + twice(3) + twice(3) + twice(14),
        compiler_params=pltpu.CompilerParams(
            collective_id=0, has_side_effects=True, vmem_limit_bytes=60 * 2**20
        ),
        name="fused",
    )(
        global_blocks, random_blocks, window_width, queries, key_heads, value_heads, output, output_grad, log_totals
    )


def solution(mesh):
    placed = (
        P(("outer", "inner"), "head"),
        P(("outer", "inner", "head"), None),
        P(("outer", "inner", "head"), None),
        P(("outer", "inner"), "head"),
        P(("outer", "inner"), "head"),
        P("head", ("outer", "inner")),
        P(("outer", "inner"), None),
        P(("outer", "inner")),
        P(),
    )
    return jax.shard_map(
        on_device,
        mesh=mesh,
        in_specs=placed,
        out_specs=(
            P(("outer", "inner"), "head"),
            P(("outer", "inner", "head"), None),
            P(("outer", "inner", "head"), None),
        ),
        check_vma=False,
    )
```

time: 1280 us -> 87.4 us (0.07)
  waiting for transfers between devices: 1040 us -> 0 us
  local copies, waits for them, and re-layouts: 104 us -> 4.1 us
  Pallas kernels: 0 us -> 81.1 us
  matrix products: 41.9 us -> 0 us
  starting transfers between devices: 41.6 us -> 0 us
  other arithmetic: 21.8 us -> 0 us
  between operations: 21.5 us -> 0.65 us
    psum x2 -> x0, waiting for transfers between devices: 1020 us -> none  [the longest x1 511 us: from_root(): return lax.psum(jnp.where(mine, value, jnp.zeros_like(value)), axis)]
    pallas_call x0 -> x1, Pallas kernels: none -> 81.1 us  [on_device(): pl.pallas_call(fused, out_shape=(shape((256, 2048), BF), shape((BLOCK, 10...]
    dot_general x21 -> x0, matrix products: 41.9 us -> none  [the longest x4 10.7 us: on_device(): jnp.einsum('bgqjk,bjkd->bqgd', score_grad, key_tiles, preferred_element_t...]
    reshape x20 -> x0, local copies, waits for them, and re-layouts: 37.1 us -> none  [the longest x1 16.4 us: on_device(): slots_out.reshape(2, outer_size, slot_cap, BLOCK, kv_width)]
    all_to_all x5 -> x0, starting transfers between devices: 29.9 us -> none  [the longest x1 9.86 us: on_device(): lax.all_to_all(slots_out.reshape(2, outer_size, slot_cap, BLOCK, kv_width...]
    unnamed x59 -> x7, local copies, waits for them, and re-layouts: 20.5 us -> 4.1 us
    all_to_all x6 -> x0, local copies, waits for them, and re-layouts: 14.8 us -> none  [the longest x1 10.1 us: on_device(): lax.all_to_all(slots_out.reshape(2, outer_size, slot_cap, BLOCK, kv_width...]
  transfers between devices with their start and end apart: 12 -> 0, of which waited for: 7 -> 0; matrix products, arithmetic and copies ran while one was open for 9% -> 0% of each run, Pallas kernels for 0% -> 0%
where the time goes in v2:
time: 87.4 us; the launch traced here: 85.8 us
  Pallas kernels  81.1 us (93%)
  local copies, waits for them, and re-layouts  4.1 us (5%)
    pallas_call x1, Pallas kernels, on_device(): pl.pallas_call(fused, out_shape=(shape((256, 2048), BF), shape((BLOCK, 10...  81.1 us
    unnamed x7, local copies, waits for them, and re-layouts  4.1 us

profile of v2, /device:TPU:8, one launch (start us, length us, event | category | flops | bytes accessed | tf_op | source)
XLA Modules:
  0.0 85.8 jit_solution(10271240752911745676)
XLA Ops:
  0.6 81.1 %fused.1 = (bf16[256,2048]{1,0:T(8,128)(2,1)}, bf16[128,1024]{1,0:T(8,128)(2,1)}, bf16[128,1024]{1,0:T(8,128)(2,1)}) custom-call(s32[2]{0:T(128)} %glob_ref.1, s32[2,3]{1,0:T(2,128)} %rand_ref.1, s32[2]{0:T(128)} %width_ref.1, bf16[256,2048]{1,0:T(8,128)(2,1)} %q_ref.1, bf16[128,1024]{1,0:T(8,128)(2,1)} %k_ref.1, bf16[128,1024]{1,0:T(8,128)(2,1)} %v_ref.1, ...), custom_call_target="tpu_custom_call" | custom-call | tf_op jit(solution)/shard_map/fused/pallas_call | solution.py:512
  81.7 0.0 copy-start.1
  81.7 2.3 %copy.15 = bf16[256,2048]{1,0:T(8,128)(2,1)} copy(bf16[256,2048]{1,0:T(8,128)(2,1)} %get-tuple-element.6) | data formatting | bytes 2097152
  84.1 0.0 copy-done.1
  84.1 0.0 copy-start
  84.1 0.7 copy.16
  84.8 0.3 copy-done
  85.1 0.7 copy.17
Async XLA Ops:
  81.7 2.4 %copy-start.1 = (bf16[128,1024]{1,0:T(8,128)(2,1)S(1)}, bf16[128,1024]{1,0:T(8,128)(2,1)}, u32[]{:S(2)}) copy-start(bf16[128,1024]{1,0:T(8,128)(2,1)} %get-tuple-element.7) | copy-start | bytes 786436
  84.1 1.0 %copy-start = (bf16[128,1024]{1,0:T(8,128)(2,1)S(1)}, bf16[128,1024]{1,0:T(8,128)(2,1)}, u32[]{:S(2)}) copy-start(bf16[128,1024]{1,0:T(8,128)(2,1)} %get-tuple-element.8) | copy-start | bytes 786436

commit v3 on v2

--- a/solution.py
+++ b/solution.py
@@ -13,6 +13,10 @@
 N = 4
 SCALE = HDIM ** (-0.5)
 LOG2E = math.log2(math.e)
+ORDER = (0, 1, 3, 2)
+UPWARD = (0, 3)
+CLOSING = (2, 1, 3, 0)
+BACKUP = (2, 3)
 YH = [(dy, dh) for dy in range(4) for dh in range(2) if (dy, dh) != (0, 0)]
 BF = jnp.bfloat16
 F32 = jnp.float32
@@ -51,7 +55,7 @@
     return device(lax.rem(z - cross + N, N), y, lax.rem(i + N - 1, N), h), spot
 
 
-def meet():
+def greet():
     barrier = pltpu.get_barrier_semaphore()
     found = [shifted(dy=dy, dh=dh) for dy, dh in YH]
     found += [shifted(dz=dz) for dz in range(1, N)]
@@ -59,7 +63,7 @@
     found += [following(N - 1)[0], preceding(0)[0]]
     for one in found:
         pl.semaphore_signal(barrier, inc=1, device_id=one, device_id_type=MESH)
-    pl.semaphore_wait(barrier, len(found))
+    return barrier, len(found)
 
 
 def remote(src, dst, send, recv, to):
@@ -86,9 +90,9 @@
 def fused(
     glob_ref, rand_ref, width_ref, q_ref, k_ref, v_ref, o_ref, g_ref, lse_ref,
     dq, dk, dv,
-    og, lseb, sbuf, intb, intr, ints, stats, qb, gb, kvu, hal, gsend, grecv,
-    dqt, acc, dhb, hrn, hrp, ent, spots, rsb, rsr, gacc, dglb, g1r, g2s, g2r, g3r, dqb, outb,
-    loc, kv_s, kv_r, q_s, q_r, st_s, st_r, it_s, it_r, ag_s, ag_r, hn_s, hn_r, hp_s, hp_r, gl_s, gl_r,
+    og, lseb, sbuf, kvh, intb, intr, ints, stats, qb, gb, kvu, hal, gsend, grecv,
+    dqt, acc, dhb, hrn, hrp, ent, rsb, rst, rsr, gacc, dglb, g1r, g2s, g2r, g3r, dqb, outb,
+    loc, kvl, kv_s, kv_r, q_s, q_r, st_s, st_r, it_s, it_r, ag_s, ag_r, hn_s, hn_r, hp_s, hp_r, gl_s, gl_r,
     dn_s, dn_r, dp_s, dp_r, rs_s, rs_r, g1_s, g1_r, g2_s, g2_r, g3_s, g3_r, dq_s, dq_r, out_s, out_r,
 ):
     z, y, i, h = place()
@@ -107,34 +111,25 @@
         pltpu.make_async_copy(q_ref.at[:, columns(y, 512)], qb.at[y], loc.at[5]),
         pltpu.make_async_copy(g_ref.at[:, columns(y, 512)], gb.at[y], loc.at[6]),
     ]
-    for one in keep + loads + stay:
+    staged = []
+    for n in range(8):
+        for side, ref in enumerate((k_ref, v_ref)):
+            staged.append(
+                pltpu.make_async_copy(ref.at[:, n * HDIM : (n + 1) * HDIM], kvh.at[n, side], kvl.at[2 * n + side])
+            )
+    for one in staged + keep + loads + stay:
         one.start()
     lane = lax.broadcasted_iota(I32, (8, 128), 1)
+    sub = lax.broadcasted_iota(I32, (8, 128), 0)
     row = jnp.zeros((8, 128), I32)
     for b in range(2):
         for r in range(3):
-            row = jnp.where(lane == b * 3 + r, rand_ref[b, r], row)
-        row = jnp.where(lane == 6 + b, width_ref[b], row)
+            slot = block_slot(rand_ref[b, r])
+            row = jnp.where((lane == b * 3 + r) & (sub == 0), slot, row)
+            row = jnp.where((lane == slot) & (sub == 1), b * 3 + r + 1, row)
+        row = jnp.where((lane == 6 + b) & (sub == 0), width_ref[b], row)
     intb[...] = row
-    meet()
-
-    it_copies = [
-        remote(intb, intr.at[y], it_s.at[dy - 1], it_r.at[dy - 1], shifted(dy=dy)) for dy in range(1, N)
-    ]
-    kv_copies = {}
-    for n, (dy, dh) in enumerate(YH):
-        to = shifted(dy=dy, dh=dh)
-        col = columns(lax.rem(h + dh, 2) * N + lax.rem(y + dy, N), HDIM)
-        for side, ref in enumerate((k_ref, v_ref)):
-            kv_copies[dy, dh, side] = remote(
-                ref.at[:, col], kvu.at[own_slot, side], kv_s.at[2 * n + side], kv_r.at[2 * n + side], to
-            )
-    for key in sorted(kv_copies, key=lambda s: ((0, 1, 3, 2)[s[0]], s[1], s[2])):
-        kv_copies[key].start()
-    for one in it_copies:
-        one.start()
-    intr[y] = row
-
+    barrier, arrivals = greet()
     for one in loads:
         one.wait()
     picker = (
@@ -147,6 +142,23 @@
         delta = lax.dot_general(picker, high, NT, preferred_element_type=F32)
         delta = delta + lax.dot_general(picker, low, NT, preferred_element_type=F32)
         sbuf[c] = jnp.concatenate([lseb[4 * c : 4 * c + 4, :] * LOG2E, delta[4:8]], axis=0)
+    pl.semaphore_wait(barrier, arrivals)
+
+    it_copies = [
+        remote(intb, intr.at[y], it_s.at[dy - 1], it_r.at[dy - 1], shifted(dy=dy)) for dy in range(1, N)
+    ]
+    kv_copies = {}
+    for one in staged:
+        one.wait()
+    for dy, dh in sorted(YH, key=lambda s: ((0, 1, 3, 2)[s[0]], s[1])):
+        n = YH.index((dy, dh))
+        to = shifted(dy=dy, dh=dh)
+        part = lax.rem(h + dh, 2) * N + lax.rem(y + dy, N)
+        kv_copies[dy, dh] = remote(kvh.at[part], kvu.at[own_slot], kv_s.at[n], kv_r.at[n], to)
+        kv_copies[dy, dh].start()
+    for one in it_copies:
+        one.start()
+    intr[y] = row
     st_copies = [
         remote(sbuf.at[lax.rem(y + dy, N)], stats.at[y], st_s.at[dy - 1], st_r.at[dy - 1], shifted(dy=dy))
         for dy in range(1, N)
@@ -155,27 +167,6 @@
         one.start()
     own_stats = pltpu.make_async_copy(sbuf.at[y], stats.at[y], loc.at[7])
     own_stats.start()
-    for one in keep:
-        one.wait()
-
-    ag_copies, hn_copies, hp_copies = [], [], []
-    for dy in (0, 1, 3, 2):
-        shard = lax.rem(y - dy + N, N)
-        for dh in range(2):
-            for side in range(2):
-                if (dy, dh) != (0, 0):
-                    kv_copies[dy, dh, side].wait_recv()
-        here = pl.ds(pl.multiple_of(z * 8 + shard * 2, 2), 2)
-        for dz in range(1, N):
-            n = dy * 3 + dz - 1
-            ag_copies.append(remote(kvu.at[here], kvu.at[here], ag_s.at[n], ag_r.at[n], shifted(dz=dz)))
-            ag_copies[-1].start()
-        to, spot = following(shard)
-        hn_copies.append(remote(kvu.at[here], hal.at[0, spot], hn_s.at[dy], hn_r.at[spot], to))
-        hn_copies[-1].start()
-        to, spot = preceding(shard)
-        hp_copies.append(remote(kvu.at[here], hal.at[1, spot], hp_s.at[dy], hp_r.at[spot], to))
-        hp_copies[-1].start()
     q_copies = {}
     for dy in (1, 3, 2):
         c = lax.rem(y + dy, N)
@@ -186,6 +177,45 @@
             )
             q_copies[dy, side].start()
 
+    for one in keep:
+        one.wait()
+
+    ag_copies, hn_copies, hp_copies = {}, [], []
+
+    def spread(dy):
+        shard = lax.rem(y - dy + N, N)
+        for dh in range(2):
+            if (dy, dh) != (0, 0):
+                kv_copies[dy, dh].wait_recv()
+        here = pl.ds(pl.multiple_of(z * 8 + shard * 2, 2), 2)
+        for dz in (1, 3):
+            n = dy * 3 + dz - 1
+            ag_copies[dy, dz] = remote(kvu.at[here], kvu.at[here], ag_s.at[n], ag_r.at[n], shifted(dz=dz))
+            ag_copies[dy, dz].start()
+        to, spot = following(shard)
+        hn_copies.append(remote(kvu.at[here], hal.at[0, spot], hn_s.at[dy], hn_r.at[spot], to))
+        hn_copies[-1].start()
+        to, spot = preceding(shard)
+        hp_copies.append(remote(kvu.at[here], hal.at[1, spot], hp_s.at[dy], hp_r.at[spot], to))
+        hp_copies[-1].start()
+
+    def pass_on(dy):
+        step = 1 if dy in UPWARD else 3
+        ag_copies[dy, step].wait_recv()
+        shard = lax.rem(y - dy + N, N)
+        here = pl.ds(pl.multiple_of(lax.rem(z - step + N, N) * 8 + shard * 2, 2), 2)
+        n = dy * 3 + 1
+        ag_copies[dy, 2] = remote(kvu.at[here], kvu.at[here], ag_s.at[n], ag_r.at[n], shifted(dz=step))
+        ag_copies[dy, 2].start()
+
+    spread(0)
+    spread(1)
+    pass_on(0)
+    spread(3)
+    pass_on(1)
+    spread(2)
+    pass_on(3)
+    pass_on(2)
     for one in it_copies + st_copies:
         one.wait_recv()
     own_stats.wait()
@@ -199,16 +229,6 @@
     for g in range(2):
         for side in range(2):
             gacc[g, side] = jnp.zeros((BLOCK, HDIM), F32)
-
-    def find(slot, carry):
-        for shard in range(N):
-            spot = 0
-            for r in range(6):
-                spot = jnp.where(block_slot(ints[shard, 0, r]) == slot, r + 1, spot)
-            spots[slot, shard] = spot
-        return carry
-
-    lax.fori_loop(0, 32, find, 0)
 
     def load_block(shard, b):
         rows = slice(b * BLOCK, (b + 1) * BLOCK)
@@ -236,6 +256,8 @@
 
     def window(k, add):
         shard = lax.rem(y - offset_of(k) + N, N)
+        remote(hal.at[0, shard], hal.at[0, shard], hn_s.at[shard], hn_r.at[shard], shifted(di=1)).wait_recv()
+        remote(hal.at[1, shard], hal.at[1, shard], hp_s.at[shard], hp_r.at[shard], shifted(di=1)).wait_recv()
         for b in range(2):
             query, grad, lse, delta = load_block(shard, b)
             width = ints[shard, 0, 6 + b]
@@ -288,10 +310,6 @@
 
     for one in stay:
         one.wait()
-    for shard in range(N):
-        remote(hal.at[0, shard], hal.at[0, shard], hn_s.at[shard], hn_r.at[shard], shifted(di=1)).wait_recv()
-        remote(hal.at[1, shard], hal.at[1, shard], hp_s.at[shard], hp_r.at[shard], shifted(di=1)).wait_recv()
-
     def early(k, carry):
         @pl.when(k > 0)
         def _():
@@ -300,10 +318,13 @@
         window(k, False)
         return carry
 
-    lax.fori_loop(0, 3, early, 0)
-
-    for one in ag_copies:
-        one.wait_recv()
+    lax.fori_loop(0, 1, early, 0)
+    lax.fori_loop(1, 3, early, 0)
+
+    for dy in range(N):
+        for dz in range(1, N):
+            if dz == 2 or dz == (3 if dy in UPWARD else 1):
+                ag_copies[dy, dz].wait_recv()
     for g in range(2):
         gsend[g] = kvu[block_slot(glob_ref[g])]
     gl_copies = [
@@ -323,7 +344,7 @@
             query, grad, lse, delta = load_block(shard, b)
             total = None
             for group in ((0, 1), (2,)):
-                slots = [block_slot(ints[shard, 0, b * 3 + r]) for r in group]
+                slots = [ints[shard, 0, b * 3 + r] for r in group]
                 pairs = [(kvu[s, 0], kvu[s, 1]) for s in slots]
                 dks, dvs, turned = attend(pairs, [lse] * len(group), query, grad, delta)
                 total = turned if total is None else total + turned
@@ -338,26 +359,51 @@
     def named(slot):
         total = None
         for shard in range(N):
-            one = ent[shard, spots[slot, shard]].astype(F32)
+            one = ent[shard, ints[shard, 1, slot]].astype(F32)
             total = one if total is None else total + one
         return total
 
-    rs_copies = []
-    for dy in range(N):
+    rs_copies = {}
+
+    def fill(dz, dy):
         shard = lax.rem(y + dy, N)
-        for dz in range(1, N):
-            to = lax.rem(z + dz, N)
-
-            def fill(b, carry, to=to, shard=shard, dz=dz):
-                rsb[dz - 1, shard, b] = named(to * 8 + shard * 2 + b).astype(BF)
+        to = lax.rem(z + dz, N)
+
+        def put(b, carry):
+            rsb[dz - 1, dy, b] = named(to * 8 + shard * 2 + b).astype(BF)
+            return carry
+
+        lax.fori_loop(0, 2, put, 0)
+
+    def rs_send(dz, dy, dst, to):
+        n = dy * 3 + dz - 1
+        rs_copies[dz, dy] = remote(rsb.at[dz - 1, dy], dst, rs_s.at[n], rs_r.at[n], to)
+        rs_copies[dz, dy].start()
+
+    def rs_first(dys):
+        for dy in dys:
+            fill(2, dy)
+            rs_send(2, dy, rst.at[dy], shifted(dz=1 if dy in BACKUP else 3))
+        for dy in dys:
+            dz = 3 if dy in BACKUP else 1
+            fill(dz, dy)
+            rs_send(dz, dy, rsr.at[dz // 2, dy], shifted(dz=dz))
+        for dy in dys:
+            fill(1 if dy in BACKUP else 3, dy)
+
+    def rs_second(dys):
+        for dy in dys:
+            dz = 1 if dy in BACKUP else 3
+            rs_copies[2, dy].wait_recv()
+
+            def join(b, carry, dz=dz, dy=dy):
+                rsb[dz - 1, dy, b] = (rsb[dz - 1, dy, b].astype(F32) + rst[dy, b].astype(F32)).astype(BF)
                 return carry
 
-            lax.fori_loop(0, 2, fill, 0)
-            n = dy * 3 + dz - 1
-            rs_copies.append(
-                remote(rsb.at[dz - 1, shard], rsr.at[dz - 1, shard], rs_s.at[n], rs_r.at[n], shifted(dz=dz))
-            )
-            rs_copies[-1].start()
+            lax.fori_loop(0, 2, join, 0)
+            rs_send(dz, dy, rsr.at[dz // 2, dy], shifted(dz=dz))
+
+    rs_first(CLOSING[:2])
 
     for one in gl_copies:
         one.wait_recv()
@@ -404,8 +450,10 @@
         window(k, True)
         return carry
 
+    lax.fori_loop(0, 3, whole, 0)
+    rs_second(CLOSING[:2])
     lax.fori_loop(3, 4, late, 0)
-    lax.fori_loop(0, N, whole, 0)
+    lax.fori_loop(3, 4, whole, 0)
 
     for g in range(2):
         dglb[2 * g] = (gacc[g, 0] * SCALE).astype(BF)
@@ -427,6 +475,7 @@
     ]
     for one in g2_copies:
         one.start()
+    rs_first(CLOSING[2:])
     for one in g2_copies:
         one.wait_recv()
     for n in range(3):
@@ -438,6 +487,7 @@
     ]
     for one in g3_copies:
         one.start()
+    rs_second(CLOSING[2:])
     for one in g3_copies:
         one.wait_recv()
     for shard in range(N):
@@ -445,19 +495,19 @@
         remote(dhb.at[1, shard], hrp.at[shard], dp_s.at[shard], dp_r.at[shard], shifted(di=1)).wait_recv()
 
     out_copies, home = [], []
-    for dy in range(N):
+    for dy in CLOSING:
         shard = lax.rem(y + dy, N)
-        for dz in range(1, N):
-            rs_copies[dy * 3 + dz - 1].wait_recv()
-
-        def close(b, carry, shard=shard):
+        rs_copies[1, dy].wait_recv()
+        rs_copies[3, dy].wait_recv()
+
+        def close(b, carry, shard=shard, dy=dy):
             block_id = ((z * N + shard) * N + i) * 2 + b
             extra = named(z * 8 + shard * 2 + b)
             for side in range(2):
                 total = acc[shard, 2 + b, side] * (SCALE if side == 0 else 1.0) + extra[side]
                 total = total + hrn[shard, b, side].astype(F32) + hrp[shard, b, side].astype(F32)
-                for n in range(3):
-                    total = total + rsr[n, shard, b, side].astype(F32)
+                for n in range(2):
+                    total = total + rsr[n, dy, b, side].astype(F32)
                 for g in range(2):
                     hit = (jnp.zeros((BLOCK, HDIM), I32) + glob_ref[g]) == block_id
                     total = total + jnp.where(hit, g3r[2 * g + side].astype(F32), 0.0)
@@ -491,11 +541,27 @@
         dq_copy(k).wait()
     for one in list(kv_copies.values()) + list(q_copies.values()) + it_copies + st_copies:
         one.wait_send()
-    for one in ag_copies + hn_copies + hp_copies + gl_copies + rs_copies + g1_copies + g2_copies + g3_copies:
+    for one in list(ag_copies.values()) + list(rs_copies.values()):
+        one.wait_send()
+    for one in hn_copies + hp_copies + gl_copies + g1_copies + g2_copies + g3_copies:
         one.wait_send()
     for shard in range(N):
         remote(dhb.at[0, shard], hrn.at[shard], dn_s.at[shard], dn_r.at[shard], shifted(di=1)).wait_send()
         remote(dhb.at[1, shard], hrp.at[shard], dp_s.at[shard], dp_r.at[shard], shifted(di=1)).wait_send()
+
+
+def hand_over(a, b, c, a_out, b_out, c_out, wide, tall, sems_in, sems_out):
+    moves = [(a.at[pl.ds(64 * n, 64)], wide.at[n], a_out.at[pl.ds(64 * n, 64)]) for n in range(4)]
+    moves += [(b, tall.at[0], b_out), (c, tall.at[1], c_out)]
+    come = [pltpu.make_async_copy(src, via, sems_in.at[n]) for n, (src, via, _) in enumerate(moves)]
+    leave = [pltpu.make_async_copy(via, dst, sems_out.at[n]) for n, (_, via, dst) in enumerate(moves)]
+    for one in come:
+        one.start()
+    for first, then in zip(come, leave):
+        first.wait()
+        then.start()
+    for one in leave:
+        one.wait()
 
 
 HBM = pl.BlockSpec(memory_space=pltpu.HBM)
@@ -509,7 +575,7 @@
     shape = jax.ShapeDtypeStruct
     tile = (BLOCK, HDIM)
     twice = lambda n: [DMA((n,)), DMA((n,))]
-    return pl.pallas_call(
+    results = pl.pallas_call(
         fused,
         out_shape=(
             shape((256, 2048), BF),
@@ -522,6 +588,7 @@
             pltpu.VMEM((2, 256, 2048), BF),
             pltpu.VMEM((16, 256), F32),
             pltpu.VMEM((N, 8, 256), F32),
+            pltpu.VMEM((8, 2) + tile, BF),
             pltpu.VMEM((8, 128), I32),
             pltpu.VMEM((N, 8, 128), I32),
             pltpu.SMEM((N, 8, 128), I32),
@@ -538,9 +605,9 @@
             pltpu.VMEM((N, 2, 2) + tile, BF),
             pltpu.VMEM((N, 2, 2) + tile, BF),
             pltpu.VMEM((N, 7, 2) + tile, BF),
-            pltpu.SMEM((32, N), I32),
             pltpu.VMEM((3, N, 2, 2) + tile, BF),
-            pltpu.VMEM((3, N, 2, 2) + tile, BF),
+            pltpu.VMEM((N, 2, 2) + tile, BF),
+            pltpu.VMEM((2, N, 2, 2) + tile, BF),
             pltpu.VMEM((2, 2) + tile, F32),
             pltpu.VMEM((4,) + tile, BF),
             pltpu.VMEM((3,) + tile, BF),
@@ -550,8 +617,9 @@
             pltpu.VMEM((N, 256, 512), BF),
             pltpu.VMEM((N, 2, 2) + tile, BF),
             DMA((12,)),
+            DMA((16,)),
         ]
-        + twice(14) + twice(6) + twice(3) + twice(3) + twice(12) + twice(4) + twice(4) + twice(3)
+        + twice(7) + twice(6) + twice(3) + twice(3) + twice(12) + twice(4) + twice(4) + twice(3)
         + twice(4) + twice(4) + twice(12) + twice(3) + twice(3) + twice(3) + twice(3) + twice(14),
         compiler_params=pltpu.CompilerParams(
             collective_id=0, has_side_effects=True, vmem_limit_bytes=60 * 2**20
@@ -560,6 +628,20 @@
     )(
         global_blocks, random_blocks, window_width, queries, key_heads, value_heads, output, output_grad, log_totals
     )
+    return pl.pallas_call(
+        hand_over,
+        out_shape=tuple(shape(one.shape, BF) for one in results),
+        in_specs=[HBM] * 3,
+        out_specs=(HBM, HBM, HBM),
+        scratch_shapes=[
+            pltpu.VMEM((4, 64, 2048), BF),
+            pltpu.VMEM((2, BLOCK, 1024), BF),
+            DMA((6,)),
+            DMA((6,)),
+        ],
+        compiler_params=pltpu.CompilerParams(vmem_limit_bytes=60 * 2**20),
+        name="hand_over",
+    )(*results)
 
 
 def solution(mesh):

time: 87.4 us -> 79.3 us (0.907); the launches traced: 85.8 us -> 79.1 us
  local copies, waits for them, and re-layouts: 4.1 us -> 0 us
  Pallas kernels: 81.1 us -> 78.5 us
    pallas_call x1, Pallas kernels: 81.1 us -> 76.3 us  [on_device(): pl.pallas_call(fused, out_shape=(shape((256, 2048), BF), shape((BLOCK, 10...]
    unnamed x7 -> x0, local copies, waits for them, and re-layouts: 4.1 us -> none
    pallas_call x0 -> x1, Pallas kernels: none -> 2.19 us  [on_device(): pl.pallas_call(hand_over, out_shape=tuple((shape(one.shape, BF) for one i...]
where the time goes in v3:
time: 79.3 us; the launch traced here: 79.1 us
  Pallas kernels  78.5 us (99%)
    pallas_call x1, Pallas kernels, on_device(): pl.pallas_call(fused, out_shape=(shape((256, 2048), BF), shape((BLOCK, 10...  76.3 us
    pallas_call x1, Pallas kernels, on_device(): pl.pallas_call(hand_over, out_shape=tuple((shape(one.shape, BF) for one i...  2.19 us

profile of v3, /device:TPU:8, one launch (start us, length us, event | category | flops | bytes accessed | tf_op | source)
XLA Modules:
  0.0 79.1 jit_solution(8921654730607978071)
XLA Ops:
  0.6 76.3 %fused.1 = (bf16[256,2048]{1,0:T(8,128)(2,1)}, bf16[128,1024]{1,0:T(8,128)(2,1)}, bf16[128,1024]{1,0:T(8,128)(2,1)}) custom-call(s32[2]{0:T(128)} %glob_ref.1, s32[2,3]{1,0:T(2,128)} %rand_ref.1, s32[2]{0:T(128)} %width_ref.1, bf16[256,2048]{1,0:T(8,128)(2,1)} %q_ref.1, bf16[128,1024]{1,0:T(8,128)(2,1)} %k_ref.1, bf16[128,1024]{1,0:T(8,128)(2,1)} %v_ref.1, ...), custom_call_target="tpu_custom_call" | custom-call | tf_op jit(solution)/shard_map/fused/pallas_call | solution.py:578
  76.9 2.2 %hand_over.1 = (bf16[256,2048]{1,0:T(8,128)(2,1)}, bf16[128,1024]{1,0:T(8,128)(2,1)}, bf16[128,1024]{1,0:T(8,128)(2,1)}) custom-call(bf16[256,2048]{1,0:T(8,128)(2,1)} %get-tuple-element.6.a, bf16[128,1024]{1,0:T(8,128)(2,1)} %get-tuple-element.7.b, bf16[128,1024]{1,0:T(8,128)(2,1)} %get-tuple-element.8.c), custom_call_target="tpu_custom_call" | custom-call | tf_op jit(solution)/shard_map/hand_over/pallas_call | solution.py:631

commit v4 on v3

--- a/solution.py
+++ b/solution.py
@@ -15,6 +15,8 @@
 LOG2E = math.log2(math.e)
 ORDER = (0, 1, 3, 2)
 UPWARD = (0, 3)
+WINDOW_GROUPS = ((0, 1), (2, 3), (4,))
+RANDOM_GROUPS = ((0, 1), (2,))
 CLOSING = (2, 1, 3, 0)
 BACKUP = (2, 3)
 YH = [(dy, dh) for dy in range(4) for dh in range(2) if (dy, dh) != (0, 0)]
@@ -89,7 +91,7 @@
 
 def fused(
     glob_ref, rand_ref, width_ref, q_ref, k_ref, v_ref, o_ref, g_ref, lse_ref,
-    dq, dk, dv,
+    dq, dkv,
     og, lseb, sbuf, kvh, intb, intr, ints, stats, qb, gb, kvu, hal, gsend, grecv,
     dqt, acc, dhb, hrn, hrp, ent, rsb, rst, rsr, gacc, dglb, g1r, g2s, g2r, g3r, dqb, outb,
     loc, kvl, kv_s, kv_r, q_s, q_r, st_s, st_r, it_s, it_r, ag_s, ag_r, hn_s, hn_r, hp_s, hp_r, gl_s, gl_r,
@@ -130,6 +132,23 @@
         row = jnp.where((lane == 6 + b) & (sub == 0), width_ref[b], row)
     intb[...] = row
     barrier, arrivals = greet()
+    pl.semaphore_wait(barrier, arrivals)
+
+    it_copies = [
+        remote(intb, intr.at[y], it_s.at[dy - 1], it_r.at[dy - 1], shifted(dy=dy)) for dy in range(1, N)
+    ]
+    kv_copies = {}
+    for one in staged:
+        one.wait()
+    for dy, dh in sorted(YH, key=lambda s: ((0, 1, 3, 2)[s[0]], s[1])):
+        n = YH.index((dy, dh))
+        to = shifted(dy=dy, dh=dh)
+        part = lax.rem(h + dh, 2) * N + lax.rem(y + dy, N)
+        kv_copies[dy, dh] = remote(kvh.at[part], kvu.at[own_slot], kv_s.at[n], kv_r.at[n], to)
+        kv_copies[dy, dh].start()
+    for one in it_copies:
+        one.start()
+    intr[y] = row
     for one in loads:
         one.wait()
     picker = (
@@ -142,23 +161,6 @@
         delta = lax.dot_general(picker, high, NT, preferred_element_type=F32)
         delta = delta + lax.dot_general(picker, low, NT, preferred_element_type=F32)
         sbuf[c] = jnp.concatenate([lseb[4 * c : 4 * c + 4, :] * LOG2E, delta[4:8]], axis=0)
-    pl.semaphore_wait(barrier, arrivals)
-
-    it_copies = [
-        remote(intb, intr.at[y], it_s.at[dy - 1], it_r.at[dy - 1], shifted(dy=dy)) for dy in range(1, N)
-    ]
-    kv_copies = {}
-    for one in staged:
-        one.wait()
-    for dy, dh in sorted(YH, key=lambda s: ((0, 1, 3, 2)[s[0]], s[1])):
-        n = YH.index((dy, dh))
-        to = shifted(dy=dy, dh=dh)
-        part = lax.rem(h + dh, 2) * N + lax.rem(y + dy, N)
-        kv_copies[dy, dh] = remote(kvh.at[part], kvu.at[own_slot], kv_s.at[n], kv_r.at[n], to)
-        kv_copies[dy, dh].start()
-    for one in it_copies:
-        one.start()
-    intr[y] = row
     st_copies = [
         remote(sbuf.at[lax.rem(y + dy, N)], stats.at[y], st_s.at[dy - 1], st_r.at[dy - 1], shifted(dy=dy))
         for dy in range(1, N)
@@ -168,7 +170,8 @@
     own_stats = pltpu.make_async_copy(sbuf.at[y], stats.at[y], loc.at[7])
     own_stats.start()
     q_copies = {}
-    for dy in (1, 3, 2):
+
+    def ask(dy):
         c = lax.rem(y + dy, N)
         for side, (ref, dst) in enumerate(((q_ref, qb), (g_ref, gb))):
             n = 2 * (dy - 1) + side
@@ -177,6 +180,7 @@
             )
             q_copies[dy, side].start()
 
+    ask(1)
     for one in keep:
         one.wait()
 
@@ -209,13 +213,12 @@
         ag_copies[dy, 2].start()
 
     spread(0)
+    ask(3)
     spread(1)
     pass_on(0)
     spread(3)
     pass_on(1)
     spread(2)
-    pass_on(3)
-    pass_on(2)
     for one in it_copies + st_copies:
         one.wait_recv()
     own_stats.wait()
@@ -263,7 +266,7 @@
             width = ints[shard, 0, 6 + b]
             block_id = ((z * N + shard) * N + i) * 2 + b
             total = None
-            for group in ((0, 1), (2, 3), (4,)):
+            for group in WINDOW_GROUPS:
                 pairs, lses = [], []
                 for e in group:
                     at = b + e - 2
@@ -319,6 +322,9 @@
         return carry
 
     lax.fori_loop(0, 1, early, 0)
+    ask(2)
+    pass_on(3)
+    pass_on(2)
     lax.fori_loop(1, 3, early, 0)
 
     for dy in range(N):
@@ -343,7 +349,7 @@
         for b in range(2):
             query, grad, lse, delta = load_block(shard, b)
             total = None
-            for group in ((0, 1), (2,)):
+            for group in RANDOM_GROUPS:
                 slots = [ints[shard, 0, b * 3 + r] for r in group]
                 pairs = [(kvu[s, 0], kvu[s, 1]) for s in slots]
                 dks, dvs, turned = attend(pairs, [lse] * len(group), query, grad, delta)
@@ -380,16 +386,20 @@
         rs_copies[dz, dy] = remote(rsb.at[dz - 1, dy], dst, rs_s.at[n], rs_r.at[n], to)
         rs_copies[dz, dy].start()
 
+    def rs_fill(dys):
+        for dy in dys:
+            fill(2, dy)
+        for dy in dys:
+            fill(3 if dy in BACKUP else 1, dy)
+        for dy in dys:
+            fill(1 if dy in BACKUP else 3, dy)
+
     def rs_first(dys):
         for dy in dys:
-            fill(2, dy)
             rs_send(2, dy, rst.at[dy], shifted(dz=1 if dy in BACKUP else 3))
         for dy in dys:
             dz = 3 if dy in BACKUP else 1
-            fill(dz, dy)
             rs_send(dz, dy, rsr.at[dz // 2, dy], shifted(dz=dz))
-        for dy in dys:
-            fill(1 if dy in BACKUP else 3, dy)
 
     def rs_second(dys):
         for dy in dys:
@@ -403,6 +413,7 @@
             lax.fori_loop(0, 2, join, 0)
             rs_send(dz, dy, rsr.at[dz // 2, dy], shifted(dz=dz))
 
+    rs_fill(CLOSING[:2])
     rs_first(CLOSING[:2])
 
     for one in gl_copies:
@@ -430,7 +441,13 @@
             for g in range(2):
                 gacc[g, 0] += dks[g]
                 gacc[g, 1] += dvs[g]
-            done = (jnp.transpose(dqt[2 * k + b] + turned) * SCALE).astype(BF)
+            dqt[2 * k + b] += turned
+        return carry
+
+    def give_query(k, carry):
+        shard = lax.rem(y - offset_of(k) + N, N)
+        for b in range(2):
+            done = (jnp.transpose(dqt[2 * k + b]) * SCALE).astype(BF)
             for j in range(4):
                 dqb[shard, b * BLOCK : (b + 1) * BLOCK, j * HDIM : (j + 1) * HDIM] = done[
                     j * BLOCK : (j + 1) * BLOCK
@@ -450,11 +467,7 @@
         window(k, True)
         return carry
 
-    lax.fori_loop(0, 3, whole, 0)
-    rs_second(CLOSING[:2])
-    lax.fori_loop(3, 4, late, 0)
-    lax.fori_loop(3, 4, whole, 0)
-
+    lax.fori_loop(0, N, whole, 0)
     for g in range(2):
         dglb[2 * g] = (gacc[g, 0] * SCALE).astype(BF)
         dglb[2 * g + 1] = gacc[g, 1].astype(BF)
@@ -464,6 +477,9 @@
     ]
     for one in g1_copies:
         one.start()
+    rs_second(CLOSING[:2])
+    lax.fori_loop(0, 3, give_query, 0)
+    rs_fill(CLOSING[2:])
     for one in g1_copies:
         one.wait_recv()
     partial = dglb[i].astype(F32)
@@ -476,6 +492,8 @@
     for one in g2_copies:
         one.start()
     rs_first(CLOSING[2:])
+    lax.fori_loop(3, 4, late, 0)
+    lax.fori_loop(3, 4, give_query, 0)
     for one in g2_copies:
         one.wait_recv()
     for n in range(3):
@@ -517,24 +535,17 @@
         lax.fori_loop(0, 2, close, 0)
         for dh in range(2):
             b = lax.rem(h + dh, 2)
-            for side, ref in enumerate((dk, dv)):
-                if (dy, dh) == (0, 0):
-                    home.append(
-                        pltpu.make_async_copy(outb.at[shard, b, side], ref.at[:, own_col], loc.at[10 + side])
+            if (dy, dh) == (0, 0):
+                home.append(pltpu.make_async_copy(outb.at[shard, b], dkv.at[h * N + y], loc.at[10]))
+                home[-1].start()
+            else:
+                n = YH.index((dy, dh))
+                out_copies.append(
+                    remote(
+                        outb.at[shard, b], dkv.at[h * N + y], out_s.at[n], out_r.at[n], shifted(dy=dy, dh=dh)
                     )
-                    home[-1].start()
-                else:
-                    n = 2 * YH.index((dy, dh)) + side
-                    out_copies.append(
-                        remote(
-                            outb.at[shard, b, side],
-                            ref.at[:, own_col],
-                            out_s.at[n],
-                            out_r.at[n],
-                            shifted(dy=dy, dh=dh),
-                        )
-                    )
-                    out_copies[-1].start()
+                )
+                out_copies[-1].start()
     for one in out_copies + home + [dq_home]:
         one.wait()
     for k in range(1, N):
@@ -550,16 +561,25 @@
         remote(dhb.at[1, shard], hrp.at[shard], dp_s.at[shard], dp_r.at[shard], shifted(di=1)).wait_send()
 
 
-def hand_over(a, b, c, a_out, b_out, c_out, wide, tall, sems_in, sems_out):
-    moves = [(a.at[pl.ds(64 * n, 64)], wide.at[n], a_out.at[pl.ds(64 * n, 64)]) for n in range(4)]
-    moves += [(b, tall.at[0], b_out), (c, tall.at[1], c_out)]
-    come = [pltpu.make_async_copy(src, via, sems_in.at[n]) for n, (src, via, _) in enumerate(moves)]
-    leave = [pltpu.make_async_copy(via, dst, sems_out.at[n]) for n, (_, via, dst) in enumerate(moves)]
+def hand_over(dq, dkv, dq_out, dk_out, dv_out, wide, tall, sems_in, sems_out):
+    come = [pltpu.make_async_copy(dq.at[pl.ds(64 * n, 64)], wide.at[n], sems_in.at[n]) for n in range(4)]
+    leave = [pltpu.make_async_copy(wide.at[n], dq_out.at[pl.ds(64 * n, 64)], sems_out.at[n]) for n in range(4)]
+    whole_in = pltpu.make_async_copy(dkv, tall, sems_in.at[4])
     for one in come:
         one.start()
+    whole_in.start()
     for first, then in zip(come, leave):
         first.wait()
         then.start()
+    whole_in.wait()
+    for n in range(8):
+        for side, ref in enumerate((dk_out, dv_out)):
+            leave.append(
+                pltpu.make_async_copy(
+                    tall.at[n, side], ref.at[:, n * HDIM : (n + 1) * HDIM], sems_out.at[4 + 2 * n + side]
+                )
+            )
+            leave[-1].start()
     for one in leave:
         one.wait()
 
@@ -579,11 +599,10 @@
         fused,
         out_shape=(
             shape((256, 2048), BF),
-            shape((BLOCK, 1024), BF),
-            shape((BLOCK, 1024), BF),
+            shape((8, 2) + tile, BF),
         ),
         in_specs=[SMEM, SMEM, SMEM] + [HBM] * 6,
-        out_specs=(HBM, HBM, HBM),
+        out_specs=(HBM, HBM),
         scratch_shapes=[
             pltpu.VMEM((2, 256, 2048), BF),
             pltpu.VMEM((16, 256), F32),
@@ -620,7 +639,7 @@
             DMA((16,)),
         ]
         + twice(7) + twice(6) + twice(3) + twice(3) + twice(12) + twice(4) + twice(4) + twice(3)
-        + twice(4) + twice(4) + twice(12) + twice(3) + twice(3) + twice(3) + twice(3) + twice(14),
+        + twice(4) + twice(4) + twice(12) + twice(3) + twice(3) + twice(3) + twice(3) + twice(7),
         compiler_params=pltpu.CompilerParams(
             collective_id=0, has_side_effects=True, vmem_limit_bytes=60 * 2**20
         ),
@@ -630,14 +649,14 @@
     )
     return pl.pallas_call(
         hand_over,
-        out_shape=tuple(shape(one.shape, BF) for one in results),
-        in_specs=[HBM] * 3,
+        out_shape=(shape((256, 2048), BF), shape((BLOCK, 1024), BF), shape((BLOCK, 1024), BF)),
+        in_specs=[HBM] * 2,
         out_specs=(HBM, HBM, HBM),
         scratch_shapes=[
             pltpu.VMEM((4, 64, 2048), BF),
-            pltpu.VMEM((2, BLOCK, 1024), BF),
-            DMA((6,)),
-            DMA((6,)),
+            pltpu.VMEM((8, 2) + tile, BF),
+            DMA((5,)),
+            DMA((20,)),
         ],
         compiler_params=pltpu.CompilerParams(vmem_limit_bytes=60 * 2**20),
         name="hand_over",

time: 79.3 us -> 74.4 us (0.938); the launches traced: 79.1 us -> 73.2 us
  Pallas kernels: 78.5 us -> 72.6 us
    pallas_call x2, Pallas kernels: 78.5 us -> 72.6 us  [the longest x1 70.2 us: on_device(): pl.pallas_call(fused, out_shape=(shape((256, 2048), BF), shape((8, 2) + t...]
where the time goes in v4:
time: 74.4 us; the launch traced here: 73.2 us
  Pallas kernels  72.6 us (98%)
    pallas_call x1, Pallas kernels, on_device(): pl.pallas_call(fused, out_shape=(shape((256, 2048), BF), shape((8, 2) + t...  70.2 us
    pallas_call x1, Pallas kernels, on_device(): pl.pallas_call(hand_over, out_shape=(shape((256, 2048), BF), shape((BLOCK...  2.36 us

profile of v4, /device:TPU:8, one launch (start us, length us, event | category | flops | bytes accessed | tf_op | source)
XLA Modules:
  0.0 73.2 jit_solution(10551999290786499036)
XLA Ops:
  0.6 70.2 %fused.1 = (bf16[256,2048]{1,0:T(8,128)(2,1)}, bf16[8,2,128,128]{3,2,1,0:T(8,128)(2,1)}) custom-call(s32[2]{0:T(128)} %glob_ref.1, s32[2,3]{1,0:T(2,128)} %rand_ref.1, s32[2]{0:T(128)} %width_ref.1, bf16[256,2048]{1,0:T(8,128)(2,1)} %q_ref.1, bf16[128,1024]{1,0:T(8,128)(2,1)} %k_ref.1, bf16[128,1024]{1,0:T(8,128)(2,1)} %v_ref.1, bf16[256,2048]{1,0:T(8,128)(2,1)} %o_ref.1, ...), custom_call_target="tpu_custom_call" | custom-call | tf_op jit(solution)/shard_map/fused/pallas_call | solution.py:598
  70.9 2.4 %hand_over.1 = (bf16[256,2048]{1,0:T(8,128)(2,1)}, bf16[128,1024]{1,0:T(8,128)(2,1)}, bf16[128,1024]{1,0:T(8,128)(2,1)}) custom-call(bf16[256,2048]{1,0:T(8,128)(2,1)} %get-tuple-element.5.dq, bf16[8,2,128,128]{3,2,1,0:T(8,128)(2,1)} %get-tuple-element.6.dkv), custom_call_target="tpu_custom_call" | custom-call | tf_op jit(solution)/shard_map/hand_over/pallas_call | solution.py:650

commit v5 on v4

--- a/solution.py
+++ b/solution.py
@@ -93,7 +93,7 @@
     glob_ref, rand_ref, width_ref, q_ref, k_ref, v_ref, o_ref, g_ref, lse_ref,
     dq, dkv,
     og, lseb, sbuf, kvh, intb, intr, ints, stats, qb, gb, kvu, hal, gsend, grecv,
-    dqt, acc, dhb, hrn, hrp, ent, rsb, rst, rsr, gacc, dglb, g1r, g2s, g2r, g3r, dqb, outb,
+    dqt, dsb, acc, dhb, hrn, hrp, ent, rsb, rst, rsr, gacc, dglb, g1r, g2s, g2r, g3r, dqb, outb,
     loc, kvl, kv_s, kv_r, q_s, q_r, st_s, st_r, it_s, it_r, ag_s, ag_r, hn_s, hn_r, hp_s, hp_r, gl_s, gl_r,
     dn_s, dn_r, dp_s, dp_r, rs_s, rs_r, g1_s, g1_r, g2_s, g2_r, g3_s, g3_r, dq_s, dq_r, out_s, out_r,
 ):
@@ -227,8 +227,6 @@
     to_scalar.wait()
     for shard in range(N):
         ent[shard, 0] = jnp.zeros((2, BLOCK, HDIM), BF)
-    for b in range(2):
-        dqt[6 + b] = jnp.zeros((HDIM, 512), F32)
     for g in range(2):
         for side in range(2):
             gacc[g, side] = jnp.zeros((BLOCK, HDIM), F32)
@@ -242,7 +240,7 @@
         delta = jnp.concatenate([tile[4 + j : 5 + j] for j in range(4)], axis=1)
         return query, grad, lse, delta
 
-    def attend(pairs, lses, query, grad, delta):
+    def attend(pairs, lses, query, grad, delta, held=None):
         count = len(pairs)
         keys = jnp.concatenate([k for k, _ in pairs], axis=0)
         values = jnp.concatenate([v for _, v in pairs], axis=0)
@@ -253,7 +251,12 @@
         score_grad = (probs * (prob_grad - delta)).astype(BF)
         value_entry = jnp.dot(probs.astype(BF), grad, preferred_element_type=F32)
         key_entry = jnp.dot(score_grad, query, preferred_element_type=F32)
-        turned = lax.dot_general(keys, score_grad, TN, preferred_element_type=F32)
+        if held is None:
+            turned = lax.dot_general(keys, score_grad, TN, preferred_element_type=F32)
+        else:
+            block, start = held
+            dsb[block, start : start + count * BLOCK] = score_grad
+            turned = None
         cut = [slice(k * BLOCK, (k + 1) * BLOCK) for k in range(count)]
         return [key_entry[c] for c in cut], [value_entry[c] for c in cut], turned
 
@@ -348,16 +351,14 @@
         shard = lax.rem(y - offset_of(k) + N, N)
         for b in range(2):
             query, grad, lse, delta = load_block(shard, b)
-            total = None
             for group in RANDOM_GROUPS:
                 slots = [ints[shard, 0, b * 3 + r] for r in group]
                 pairs = [(kvu[s, 0], kvu[s, 1]) for s in slots]
-                dks, dvs, turned = attend(pairs, [lse] * len(group), query, grad, delta)
-                total = turned if total is None else total + turned
+                held = (2 * k + b, (2 + group[0]) * BLOCK)
+                dks, dvs, _ = attend(pairs, [lse] * len(group), query, grad, delta, held)
                 for r, dk_e, dv_e in zip(group, dks, dvs):
                     ent[shard, 1 + b * 3 + r, 0] = (dk_e * SCALE).astype(BF)
                     ent[shard, 1 + b * 3 + r, 1] = dv_e.astype(BF)
-            dqt[2 * k + b] += total
         return carry
 
     lax.fori_loop(0, N, random, 0)
@@ -437,17 +438,21 @@
         for b in range(2):
             query, grad, lse, delta = load_block(shard, b)
             pairs = [(grecv[globe[g], g, 0], grecv[globe[g], g, 1]) for g in range(2)]
-            dks, dvs, turned = attend(pairs, [lse] * 2, query, grad, delta)
+            dks, dvs, _ = attend(pairs, [lse] * 2, query, grad, delta, (2 * k + b, 0))
             for g in range(2):
                 gacc[g, 0] += dks[g]
                 gacc[g, 1] += dvs[g]
-            dqt[2 * k + b] += turned
         return carry
 
     def give_query(k, carry):
         shard = lax.rem(y - offset_of(k) + N, N)
         for b in range(2):
-            done = (jnp.transpose(dqt[2 * k + b]) * SCALE).astype(BF)
+            keys = [grecv[globe[g], g, 0] for g in range(2)]
+            keys += [kvu[ints[shard, 0, b * 3 + r], 0] for r in range(3)]
+            turned = lax.dot_general(
+                jnp.concatenate(keys, axis=0), dsb[2 * k + b], TN, preferred_element_type=F32
+            )
+            done = (jnp.transpose(dqt[2 * k + b] + turned) * SCALE).astype(BF)
             for j in range(4):
                 dqb[shard, b * BLOCK : (b + 1) * BLOCK, j * HDIM : (j + 1) * HDIM] = done[
                     j * BLOCK : (j + 1) * BLOCK
@@ -464,7 +469,7 @@
         return carry
 
     def late(k, carry):
-        window(k, True)
+        window(k, False)
         return carry
 
     lax.fori_loop(0, N, whole, 0)
@@ -619,6 +624,7 @@
             pltpu.VMEM((2, 2) + tile, BF),
             pltpu.VMEM((N, 2, 2) + tile, BF),
             pltpu.VMEM((8, HDIM, 512), F32),
+            pltpu.VMEM((8, 5 * BLOCK, 512), BF),
             pltpu.VMEM((N, 6, 2) + tile, F32),
             pltpu.VMEM((2, N, 2, 2) + tile, BF),
             pltpu.VMEM((N, 2, 2) + tile, BF),

time: 74.4 us -> 74.4 us (level)
  no operation moved by 1% of the time
where the time goes in v5:
time: 74.4 us; the launch traced here: 72.9 us
  Pallas kernels  72.3 us (97%)
    pallas_call x1, Pallas kernels, on_device(): pl.pallas_call(fused, out_shape=(shape((256, 2048), BF), shape((8, 2) + t...  69.9 us
    pallas_call x1, Pallas kernels, on_device(): pl.pallas_call(hand_over, out_shape=(shape((256, 2048), BF), shape((BLOCK...  2.36 us

profile of v5, /device:TPU:8, one launch (start us, length us, event | category | flops | bytes accessed | tf_op | source)
XLA Modules:
  0.0 72.9 jit_solution(3242080047159997802)
XLA Ops:
  0.6 69.9 %fused.1 = (bf16[256,2048]{1,0:T(8,128)(2,1)}, bf16[8,2,128,128]{3,2,1,0:T(8,128)(2,1)}) custom-call(s32[2]{0:T(128)} %glob_ref.1, s32[2,3]{1,0:T(2,128)} %rand_ref.1, s32[2]{0:T(128)} %width_ref.1, bf16[256,2048]{1,0:T(8,128)(2,1)} %q_ref.1, bf16[128,1024]{1,0:T(8,128)(2,1)} %k_ref.1, bf16[128,1024]{1,0:T(8,128)(2,1)} %v_ref.1, bf16[256,2048]{1,0:T(8,128)(2,1)} %o_ref.1, ...), custom_call_target="tpu_custom_call" | custom-call | tf_op jit(solution)/shard_map/fused/pallas_call | solution.py:603
  70.6 2.4 %hand_over.1 = (bf16[256,2048]{1,0:T(8,128)(2,1)}, bf16[128,1024]{1,0:T(8,128)(2,1)}, bf16[128,1024]{1,0:T(8,128)(2,1)}) custom-call(bf16[256,2048]{1,0:T(8,128)(2,1)} %get-tuple-element.5.dq, bf16[8,2,128,128]{3,2,1,0:T(8,128)(2,1)} %get-tuple-element.6.dkv), custom_call_target="tpu_custom_call" | custom-call | tf_op jit(solution)/shard_map/hand_over/pallas_call | solution.py:656

commit v6 on v4

--- a/solution.py
+++ b/solution.py
@@ -18,7 +18,6 @@
 WINDOW_GROUPS = ((0, 1), (2, 3), (4,))
 RANDOM_GROUPS = ((0, 1), (2,))
 CLOSING = (2, 1, 3, 0)
-BACKUP = (2, 3)
 YH = [(dy, dh) for dy in range(4) for dh in range(2) if (dy, dh) != (0, 0)]
 BF = jnp.bfloat16
 F32 = jnp.float32
@@ -93,7 +92,7 @@
     glob_ref, rand_ref, width_ref, q_ref, k_ref, v_ref, o_ref, g_ref, lse_ref,
     dq, dkv,
     og, lseb, sbuf, kvh, intb, intr, ints, stats, qb, gb, kvu, hal, gsend, grecv,
-    dqt, acc, dhb, hrn, hrp, ent, rsb, rst, rsr, gacc, dglb, g1r, g2s, g2r, g3r, dqb, outb,
+    dqt, acc, dhb, hrn, hrp, ent, rsb, rsr, gacc, dglb, g1r, g2s, g2r, g3r, dqb, outb,
     loc, kvl, kv_s, kv_r, q_s, q_r, st_s, st_r, it_s, it_r, ag_s, ag_r, hn_s, hn_r, hp_s, hp_r, gl_s, gl_r,
     dn_s, dn_r, dp_s, dp_r, rs_s, rs_r, g1_s, g1_r, g2_s, g2_r, g3_s, g3_r, dq_s, dq_r, out_s, out_r,
 ):
@@ -388,30 +387,13 @@
 
     def rs_fill(dys):
         for dy in dys:
-            fill(2, dy)
-        for dy in dys:
-            fill(3 if dy in BACKUP else 1, dy)
-        for dy in dys:
-            fill(1 if dy in BACKUP else 3, dy)
+            for dz in range(1, N):
+                fill(dz, dy)
 
     def rs_first(dys):
         for dy in dys:
-            rs_send(2, dy, rst.at[dy], shifted(dz=1 if dy in BACKUP else 3))
-        for dy in dys:
-            dz = 3 if dy in BACKUP else 1
-            rs_send(dz, dy, rsr.at[dz // 2, dy], shifted(dz=dz))
-
-    def rs_second(dys):
-        for dy in dys:
-            dz = 1 if dy in BACKUP else 3
-            rs_copies[2, dy].wait_recv()
-
-            def join(b, carry, dz=dz, dy=dy):
-                rsb[dz - 1, dy, b] = (rsb[dz - 1, dy, b].astype(F32) + rst[dy, b].astype(F32)).astype(BF)
-                return carry
-
-            lax.fori_loop(0, 2, join, 0)
-            rs_send(dz, dy, rsr.at[dz // 2, dy], shifted(dz=dz))
+            for dz in (2, 1, 3):
+                rs_send(dz, dy, rsr.at[dz - 1, dy], shifted(dz=dz))
 
     rs_fill(CLOSING[:2])
     rs_first(CLOSING[:2])
@@ -477,7 +459,6 @@
     ]
     for one in g1_copies:
         one.start()
-    rs_second(CLOSING[:2])
     lax.fori_loop(0, 3, give_query, 0)
     rs_fill(CLOSING[2:])
     for one in g1_copies:
@@ -505,7 +486,6 @@
     ]
     for one in g3_copies:
         one.start()
-    rs_second(CLOSING[2:])
     for one in g3_copies:
         one.wait_recv()
     for shard in range(N):
@@ -515,8 +495,8 @@
     out_copies, home = [], []
     for dy in CLOSING:
         shard = lax.rem(y + dy, N)
-        rs_copies[1, dy].wait_recv()
-        rs_copies[3, dy].wait_recv()
+        for dz in range(1, N):
+            rs_copies[dz, dy].wait_recv()
 
         def close(b, carry, shard=shard, dy=dy):
             block_id = ((z * N + shard) * N + i) * 2 + b
@@ -524,7 +504,7 @@
             for side in range(2):
                 total = acc[shard, 2 + b, side] * (SCALE if side == 0 else 1.0) + extra[side]
                 total = total + hrn[shard, b, side].astype(F32) + hrp[shard, b, side].astype(F32)
-                for n in range(2):
+                for n in range(3):
                     total = total + rsr[n, dy, b, side].astype(F32)
                 for g in range(2):
                     hit = (jnp.zeros((BLOCK, HDIM), I32) + glob_ref[g]) == block_id
@@ -625,8 +605,7 @@
             pltpu.VMEM((N, 2, 2) + tile, BF),
             pltpu.VMEM((N, 7, 2) + tile, BF),
             pltpu.VMEM((3, N, 2, 2) + tile, BF),
-            pltpu.VMEM((N, 2, 2) + tile, BF),
-            pltpu.VMEM((2, N, 2, 2) + tile, BF),
+            pltpu.VMEM((3, N, 2, 2) + tile, BF),
             pltpu.VMEM((2, 2) + tile, F32),
             pltpu.VMEM((4,) + tile, BF),
             pltpu.VMEM((3,) + tile, BF),

time: 74.4 us -> 76.2 us (1.024); the launches traced: 73.2 us -> 76 us
  Pallas kernels: 72.6 us -> 75.4 us
    pallas_call x1, Pallas kernels: 70.2 us -> 73 us  [on_device(): pl.pallas_call(fused, out_shape=(shape((256, 2048), BF), shape((8, 2) + t...]
where the time goes in v6:
time: 76.2 us; the launch traced here: 76 us
  Pallas kernels  75.4 us (99%)
    pallas_call x1, Pallas kernels, on_device(): pl.pallas_call(fused, out_shape=(shape((256, 2048), BF), shape((8, 2) + t...  73 us
    pallas_call x1, Pallas kernels, on_device(): pl.pallas_call(hand_over, out_shape=(shape((256, 2048), BF), shape((BLOCK...  2.36 us

profile of v6, /device:TPU:8, one launch (start us, length us, event | category | flops | bytes accessed | tf_op | source)
XLA Modules:
  0.0 76.0 jit_solution(8448461543255986107)
XLA Ops:
  0.6 73.0 %fused.1 = (bf16[256,2048]{1,0:T(8,128)(2,1)}, bf16[8,2,128,128]{3,2,1,0:T(8,128)(2,1)}) custom-call(s32[2]{0:T(128)} %glob_ref.1, s32[2,3]{1,0:T(2,128)} %rand_ref.1, s32[2]{0:T(128)} %width_ref.1, bf16[256,2048]{1,0:T(8,128)(2,1)} %q_ref.1, bf16[128,1024]{1,0:T(8,128)(2,1)} %k_ref.1, bf16[128,1024]{1,0:T(8,128)(2,1)} %v_ref.1, bf16[256,2048]{1,0:T(8,128)(2,1)} %o_ref.1, ...), custom_call_target="tpu_custom_call" | custom-call | tf_op jit(solution)/shard_map/fused/pallas_call | solution.py:578
  73.7 2.4 %hand_over.1 = (bf16[256,2048]{1,0:T(8,128)(2,1)}, bf16[128,1024]{1,0:T(8,128)(2,1)}, bf16[128,1024]{1,0:T(8,128)(2,1)}) custom-call(bf16[256,2048]{1,0:T(8,128)(2,1)} %get-tuple-element.5.dq, bf16[8,2,128,128]{3,2,1,0:T(8,128)(2,1)} %get-tuple-element.6.dkv), custom_call_target="tpu_custom_call" | custom-call | tf_op jit(solution)/shard_map/hand_over/pallas_call | solution.py:629
